TPU v7x, 32 devices: a whole 2x2x4 slice. The times are simulated.
32 devices in a mesh: row: 8 (over y, x, core), col: 4 (over z).
Axes of the slice: x: 2, y: 2, z: 4, core: 2. Of those that a mesh axis runs over, the one named last changes fastest.
Arguments:
- amplitudes: bfloat16 [1024, 32768], P('row', 'col'), may hold values from -6 to 6
- integrals: bfloat16 [32768, 32768], P('col', 'row'), may hold values from -0.0390625 to 0.0390625
- tile_mask: int32 [256, 256], P('col', 'row'), may hold values 0 or 1
- driving: bfloat16 [1024, 32768], P('col', 'row'), may hold values from -6 to 6
- occupied_energy: float32 [1024], P('col'), may hold values from -1.5 to -0.5
- virtual_energy: float32 [32768], P('row'), may hold values from 0.5 to 2.5
Outputs:
- update: float32 [1024, 32768], P('col', 'row')
All inputs are finite; a program needn't handle non-finite values. No bound on the sum of `tile_mask` on one device may be relied on, other than what follows from the above.
Results may differ from a plain program's by a relative error of at most 0.0003.
Values may be sent and summed in bfloat16 or wider, within the bound.
No kernel may reach another device: no remote copies, remote signals or barrier semaphores. Data moves between devices by JAX's collectives and lax.ppermute only.
A program may use at most 256 MiB of HBM per device.

v0:
```python
import jax
import jax.numpy as jnp
from jax import lax
from jax.sharding import PartitionSpec as P


def shards(amplitudes, integrals, tile_mask, driving, occupied_energy, virtual_energy):
    tiles_in = tile_mask.shape[0]
    tiles_out = tile_mask.shape[1]
    tile_size = integrals.shape[0] // tiles_in
    shaped = integrals.reshape(tiles_in, tile_size, tiles_out, tile_size)
    masked = (shaped * tile_mask.astype(jnp.bfloat16)[:, None, :, None]).reshape(integrals.shape)
    partial_sum = jnp.dot(
        lax.all_gather(amplitudes, "row", axis=0, tiled=True),
        masked,
        preferred_element_type=jnp.float32,
    )
    ladder = lax.psum_scatter(partial_sum, "col", scatter_dimension=0, tiled=True)
    denom = virtual_energy[None, :] - occupied_energy[:, None]
    return (driving.astype(jnp.float32) + ladder) / denom


def solution(mesh):
    in_specs = (
        P("row", "col"),
        P("col", "row"),
        P("col", "row"),
        P("col", "row"),
        P("col"),
        P("row"),
    )
    out_specs = P("col", "row")
    return jax.shard_map(shards, mesh=mesh, in_specs=in_specs, out_specs=out_specs, check_vma=False)
```

profile of v0, /device:TPU:0, one launch (start us, length us, event | category | flops | bytes accessed | tf_op | source)
XLA Modules:
  0.0 537.8 jit_solution(5261648317675099673)
XLA Ops:
  6.5 0.0 all-gather.2.cloned.1.call-start
  6.5 0.7 all-gather.2.cloned.1.call-update
  7.3 0.0 reduce-scatter.2.cloned.1.call-start
  7.3 0.7 convert_element_type.7
  8.0 0.1 copy.8
  8.1 93.7 %all-gather.2.cloned.1.call-done = bf16[1024,8192]{1,0:T(8,128)(2,1)} async-done(((bf16[128,8192]{1,0:T(8,128)(2,1)}), bf16[1024,8192]{1,0:T(8,128)(2,1)}) %all-gather.2.cloned.1.call-update) | async-done | bytes 16777232 | tf_op jit(solution)/shard_map/all_gather | solution.py:14
  101.8 21.2 %mul.11 = bf16[64,128,32,128]{3,2,1,0:T(8,128)(2,1)} broadcast(bf16[64,32]{1,0:T(8,128)(2,1)S(1)} %copy.8), dimensions={0,2} | broadcast | bytes 67112960 | tf_op jit(solution)/shard_map/mul | solution.py:12
  123.0 117.9 %fusion.2 = f32[1024,4096]{0,1:T(8,128)} fusion(bf16[1024,8192]{1,0:T(8,128)(2,1)} %all-gather.2.cloned.1.call-done, bf16[8192,4096]{1,0:T(8,128)(2,1)} %param.7, bf16[1024,8,32,128]{3,2,1,0:T(8,128)(2,1)} %bitcast.2), kind=kOutput, calls=%fused_computation.3 | convolution fusion | flops 68753031168 | bytes 167772160 | tf_op jit(solution)/shard_map/dot_general | solution.py:13
  240.9 0.0 copy-start
  240.9 0.0 copy-start.1
  240.9 0.0 reduce-scatter.2.cloned.1.call-update
  240.9 3.3 copy.7
  244.2 277.2 %reduce-scatter.2.cloned.1.call-done = f32[256,4096]{0,1:T(8,128)} async-done(((f32[1024,4096]{0,1:T(8,128)}), f32[256,4096]{0,1:T(8,128)}) %reduce-scatter.2.cloned.1.call-update) | async-done | bytes 4194320 | tf_op jit(solution)/shard_map/reduce_scatter | solution.py:18
  521.4 0.0 copy-done
  521.4 0.0 copy-done.1
  521.4 4.0 subtract_divide_fusion
  525.4 5.6 %copy.9 = f32[256,4096]{1,0:T(8,128)} copy(f32[256,4096]{0,1:T(8,128)} %subtract_divide_fusion) | data formatting | bytes 8388608 | tf_op jit(solution)/shard_map/div | solution.py:20
Async XLA Ops:
  6.5 95.3 %all-gather.2.cloned.1.call-start = ((), (), s32[]{:S(2)}) async-start(), calls=%async_computation.1 | async-start | bytes 18874368 | tf_op jit(solution)/shard_map/all_gather | solution.py:14
  7.3 514.1 %reduce-scatter.2.cloned.1.call-start = ((), (), s32[]{:S(2)}) async-start(), calls=%async_computation.2 | async-start | bytes 20971520 | tf_op jit(solution)/shard_map/reduce_scatter | solution.py:18
  240.9 280.5 %copy-start = (f32[4096]{0:T(1024)S(1)}, f32[4096]{0:T(1024)}, u32[]{:S(2)}) copy-start(f32[4096]{0:T(1024)} %param.11) | copy-start | bytes 49156
  240.9 280.5 %copy-start.1 = (f32[256]{0:T(256)S(1)}, f32[256]{0:T(256)}, u32[]{:S(2)}) copy-start(f32[256]{0:T(256)} %param.10) | copy-start | bytes 3076
Sparse Core Ops, SparseCore 0:
  9.2 92.5 all-gather.1
  241.0 280.2 reduce-scatter.1
where the time goes:
time: 538 us
  waiting for transfers between devices  372 us (69%)
  matrix products  118 us (22%)
  local copies, waits for them, and re-layouts  30.1 us (6%)
  between operations  13.4 us (2%)
    reduce_scatter x1, waiting for transfers between devices, shards(): lax.psum_scatter(partial_sum, 'col', scatter_dimension=0, tiled=True)  277 us
    dot_general x1, matrix products, shards(): jnp.dot(lax.all_gather(amplitudes, 'row', axis=0, tiled=True), masked, pr...  118 us
    all_gather x1, waiting for transfers between devices, shards(): lax.all_gather(amplitudes, 'row', axis=0, tiled=True)  93.7 us
    mul x1, local copies, waits for them, and re-layouts, shards(): shaped * tile_mask.astype(jnp.bfloat16)[:, None, :, None]  21.2 us
  transfers between devices with their start and end apart: 2, of which 2 were waited for; matrix products, arithmetic and copies ran while one was open for 1% of the time, Pallas kernels for 0%

commit v1 on v0

v1 whole, which is shorter than its diff:
```python
import functools
import jax
import jax.numpy as jnp
from jax import lax
from jax.experimental import pallas as pl
from jax.experimental.pallas import tpu as pltpu
from jax.sharding import PartitionSpec as P

MIB = 2**20


def product_kernel(pieces, waits, slot_ref, *refs):
    sources = refs[: len(pieces)]
    integrals_ref, mask_ref, out_ref, rows, masked, sems = refs[len(pieces) + waits :]

    @pl.when(pl.program_id(0) == 0)
    def _():
        copies = []
        for ref, count in zip(sources, pieces):
            for k in range(count):
                g = len(copies)
                source = ref.at[k] if count > 1 else ref
                copies.append(pltpu.make_async_copy(source, rows.at[slot_ref[g]], sems.at[g]))
        for copy in copies:
            copy.start()
        for copy in copies:
            copy.wait()

    tile = masked.shape[0] // mask_ref.shape[0]
    for t in range(mask_ref.shape[0]):
        part = slice(t * tile, (t + 1) * tile)
        masked[part, :] = integrals_ref[part, :] * mask_ref[t : t + 1, :]
    every = rows[...].reshape(rows.shape[0] * rows.shape[1], rows.shape[2])
    total = jnp.dot(every, masked[...], preferred_element_type=jnp.float32)
    out_ref[...] = total.reshape(out_ref.shape)


def product(arrays, slots, integrals, mask, first, width, block, waits):
    m, depth = arrays[0].shape[-2:]
    pieces = [a.shape[0] if a.ndim == 3 else 1 for a in arrays]
    devices, tiles = sum(pieces), mask.shape[0]
    grid_spec = pltpu.PrefetchScalarGridSpec(
        num_scalar_prefetch=1,
        grid=(width // block,),
        in_specs=[pl.BlockSpec(memory_space=pl.ANY)] * (len(arrays) + len(waits))
        + [
            pl.BlockSpec((depth, block), lambda n, s: (0, first // block + n)),
            pl.BlockSpec((tiles, block), lambda n, s: (0, first // block + n)),
        ],
        out_specs=pl.BlockSpec((devices, m, block), lambda n, s: (0, 0, n)),
        scratch_shapes=[
            pltpu.VMEM((devices, m, depth), jnp.bfloat16),
            pltpu.VMEM((depth, block), jnp.bfloat16),
            pltpu.SemaphoreType.DMA((devices,)),
        ],
    )
    return pl.pallas_call(
        functools.partial(product_kernel, pieces, len(waits)),
        grid_spec=grid_spec,
        out_shape=jax.ShapeDtypeStruct((devices, m, width), jnp.float32),
        compiler_params=pltpu.CompilerParams(vmem_limit_bytes=56 * MIB),
        cost_estimate=pl.CostEstimate(
            flops=2 * devices * m * depth * width,
            bytes_accessed=2 * depth * width + 4 * devices * m * width,
            transcendentals=0,
        ),
    )(slots, *arrays, *waits, integrals, mask)


def gather(own, rows):
    swap = [(i, i ^ 1) for i in range(rows)]
    others = [lax.ppermute(own, "row", [(i, i ^ q) for i in range(rows)]) for q in range(2, rows, 2)]
    pieces = [own, lax.ppermute(own, "row", swap)]
    for other in others:
        pieces += [other, lax.ppermute(other, "row", swap)]
    return pieces


def send(values, cols, edge):
    pairs = [(edge, edge + 1), (cols - 1 - edge, cols - 2 - edge)]
    return lax.ppermute(values, "col", pairs)


def after(value, others):
    return lax.optimization_barrier((value, *others))[0]


class Chain:
    def __init__(self, sums, cols, split):
        self.sums, self.cols, self.last = sums, cols, cols - 1
        self.groups = [(s, s + 1) for s in range(cols - 1)] if split else [(0, cols - 1)]
        self.came, self.ends = {}, []

    def advance(self, edge, order):
        last, came = self.last, {}
        for low, high in self.groups:
            at = max(low, edge)
            if at >= high:
                continue
            if edge < self.cols // 2:
                values = self.sums[at:high]
            else:
                values = jnp.flip(self.sums[last - high : last - at], 0)
            if edge:
                first, received = self.came[at - 1]
                received = after(received, order)
                values = values + received[at - 1 - first : high - 1 - first].astype(jnp.float32)
            values = values.astype(jnp.float16)
            order = [values]
            received = send(values, self.cols, edge)
            for k in range(at, high):
                came[k] = (at, received)
        self.came = came
        self.ends.append(received)
        return order

    def total(self):
        total = self.sums[self.last]
        for received in self.ends:
            total = total + received[-1].astype(jnp.float32)
        return total


def plan(local):
    if local == 128:
        return ((32, False, 1), (32, True, 1), (64, True, 2))
    return ((local, True, 1),)


def shards(rows, cols, amplitudes, integrals, tile_mask, driving, occupied_energy, virtual_energy):
    local, depth = amplitudes.shape
    width = integrals.shape[1]
    share = rows // cols
    me, place = lax.axis_index("row"), lax.axis_index("col")
    mask = jnp.repeat(tile_mask.astype(jnp.bfloat16), width // tile_mask.shape[1], axis=1)

    lower = place < cols // 2
    near = jnp.where(lower, place, cols - 1 - place)

    def slot_of(device):
        target = device // share
        target = jnp.where(lower, target, cols - 1 - target)
        return jnp.remainder(2 * cols - 1 + near - target, cols) * share + device % share

    device = jnp.arange(rows, dtype=jnp.int32)
    slots_all, slots_xor = slot_of(device), slot_of(jnp.bitwise_xor(device, me))

    driving = driving.reshape(share, local, width)
    occupied = occupied_energy.reshape(share, local, 1)
    layout = plan(local)
    count = sum(chunks for _, _, chunks in layout)
    chains, order, begun, offset, where = [], [], [], 0, []
    for m, whole, chunks in layout:
        part = slice(offset, offset + m)
        offset += m
        own = after(amplitudes[part], begun)
        if whole:
            arrays, slots = [lax.all_gather(own, "row", axis=0)], slots_all
        else:
            arrays, slots = gather(own, rows), slots_xor
            begun = arrays[2::2]
        chunk = width // chunks
        for c in range(chunks):
            at = c * chunk
            sums = product(arrays, after(slots, order), integrals, mask, at, chunk, min(chunk, 512), [])
            split = cols == 4 and len(chains) == count - 1
            chains.append(Chain(sums.reshape(cols, share, m, chunk), cols, split))
            where.append((part, slice(at, at + chunk)))
            for edge, chain in enumerate(chains[: -cols : -1]):
                order = chain.advance(edge, order)
    for late in range(1, cols - 1):
        for edge in range(late, cols - 1):
            if edge - late < len(chains):
                order = chains[late - edge - 1].advance(edge, order)

    outs = {}
    for (part, span), chain in zip(where, chains):
        denom = virtual_energy[None, None, span] - occupied[:, part]
        value = (driving[:, part, span].astype(jnp.float32) + chain.total()) / denom
        outs.setdefault(part.start, []).append(value)
    outs = [jnp.concatenate(parts, axis=2) for parts in outs.values()]
    return jnp.concatenate(outs, axis=1).reshape(share * local, width)


def solution(mesh):
    in_specs = (
        P("row", "col"),
        P("col", "row"),
        P("col", "row"),
        P("col", "row"),
        P("col"),
        P("row"),
    )
    fn = functools.partial(shards, mesh.shape["row"], mesh.shape["col"])
    return jax.shard_map(fn, mesh=mesh, in_specs=in_specs, out_specs=P("col", "row"), check_vma=False)
```

time: 538 us -> 284 us (0.53)
  waiting for transfers between devices: 372 us -> 72.9 us
  Pallas kernels: 0 us -> 123 us
  matrix products: 118 us -> 0 us
  starting transfers between devices: 0.04 us -> 34.6 us
  other arithmetic: 4.71 us -> 28 us
  local copies, waits for them, and re-layouts: 30.1 us -> 11.7 us
    reduce_scatter x1 -> x0, waiting for transfers between devices: 277 us -> none  [shards(): lax.psum_scatter(partial_sum, 'col', scatter_dimension=0, tiled=True)]
    pallas_call x0 -> x4, Pallas kernels: none -> 123 us  [product(): pl.pallas_call(functools.partial(product_kernel, pieces, len(waits)), gri...]
    dot_general x1 -> x0, matrix products: 118 us -> none  [shards(): jnp.dot(lax.all_gather(amplitudes, 'row', axis=0, tiled=True), masked, pr...]
    all_gather x1 -> x2, waiting for transfers between devices: 93.7 us -> 0.83 us  [shards(): arrays, slots = ([lax.all_gather(own, 'row', axis=0)], slots_all)]
    ppermute x0 -> x22, waiting for transfers between devices: none -> 72 us  [the longest x15 46.8 us: send(): return lax.ppermute(values, 'col', pairs)]
    ppermute x0 -> x22, starting transfers between devices: none -> 34.5 us  [the longest x15 29 us: send(): return lax.ppermute(values, 'col', pairs)]
    mul x1 -> x0, local copies, waits for them, and re-layouts: 21.2 us -> none  [shards(): shaped * tile_mask.astype(jnp.bfloat16)[:, None, :, None]]
    convert_element_type x1 -> x11, other arithmetic: 0.72 us -> 13.8 us  [the longest x10 13.8 us: advance(): values = values.astype(jnp.float16)]
  transfers between devices with their start and end apart: 2 -> 24, of which waited for: 2 -> 10; matrix products, arithmetic and copies ran while one was open for 1% -> 9% of each run, Pallas kernels for 0% -> 43%
where the time goes in v1:
time: 284 us
  Pallas kernels  123 us (43%)
  waiting for transfers between devices  72.9 us (26%)
  starting transfers between devices  34.6 us (12%)
  other arithmetic  28 us (10%)
  between operations  13.8 us (5%)
  local copies, waits for them, and re-layouts  11.7 us (4%)
    pallas_call x4, Pallas kernels, product(): pl.pallas_call(functools.partial(product_kernel, pieces, len(waits)), gri...  123 us
    ppermute x15, waiting for transfers between devices, send(): return lax.ppermute(values, 'col', pairs)  46.8 us
    ppermute x15, starting transfers between devices, send(): return lax.ppermute(values, 'col', pairs)  29 us
    ppermute x3, waiting for transfers between devices, gather(): lax.ppermute(own, 'row', [(i, i ^ q) for i in range(rows)])  23.1 us
    convert_element_type x10, other arithmetic, advance(): values = values.astype(jnp.float16)  13.8 us
    unnamed x37, local copies, waits for them, and re-layouts  7.79 us
    another operation x3, other arithmetic  6.11 us
  transfers between devices with their start and end apart: 24, of which 10 were waited for; matrix products, arithmetic and copies ran while one was open for 9% of the time, Pallas kernels for 43%

profile of v1, /device:TPU:0, one launch (start us, length us, event | category | flops | bytes accessed | tf_op | source)
XLA Modules:
  0.0 283.7 jit_solution(16386303276911112668)
XLA Ops:
  6.5 2.2 fusion.36
  8.8 2.9 %collective-permute-start.1 = (bf16[32,8192]{1,0:T(8,128)(2,1)S(1)}, bf16[32,8192]{1,0:T(8,128)(2,1)S(1)}, u32[]{:S(2)}, u32[]{:S(2)}) collective-permute-start(bf16[32,8192]{1,0:T(8,128)(2,1)S(1)} %get-tuple-element.41.refs_0_), channel_id=1, source_target_pairs={{0,8},{4,12},{8,0},{12,4},{16,24},{20,28},{24,16},{28,20},{1,9},{5... | collective-permute-start | bytes 1572872 | tf_op jit(solution)/shard_map/ppermute | solution.py:72
  11.7 1.5 collective-permute-start.3
  13.2 11.2 %collective-permute-done.1.refs_2_ = bf16[32,8192]{1,0:T(8,128)(2,1)S(1)} collective-permute-done((bf16[32,8192]{1,0:T(8,128)(2,1)S(1)}, bf16[32,8192]{1,0:T(8,128)(2,1)S(1)}, u32[]{:S(2)}, u32[]{:S(2)}) %collective-permute-start.1) | collective-permute-done | bytes 524320 | tf_op jit(solution)/shard_map/ppermute | solution.py:72
  24.5 11.9 %collective-permute-done.3.refs_4_ = bf16[32,8192]{1,0:T(8,128)(2,1)S(1)} collective-permute-done((bf16[32,8192]{1,0:T(8,128)(2,1)S(1)}, bf16[32,8192]{1,0:T(8,128)(2,1)S(1)}, u32[]{:S(2)}, u32[]{:S(2)}) %collective-permute-start.3) | collective-permute-done | bytes 524320 | tf_op jit(solution)/shard_map/ppermute | solution.py:72
  45.8 32.8 %shard_map.64 = f32[8,32,4096]{2,1,0:T(8,128)} custom-call(s32[8]{0:T(128)} %fusion.29.slot_ref, bf16[32,8192]{1,0:T(8,128)(2,1)} %copy-done.5, bf16[32,8192]{1,0:T(8,128)(2,1)} %copy-done.11, bf16[32,8192]{1,0:T(8,128)(2,1)} %copy-done.8, bf16[32,8192]{1,0:T(8,128)(2,1)} %copy-done.12, bf16[32,8192]{1,0:T(8,128)(2,1)} %copy-done.9, ...), custom_call_target="tpu_custom_call" | custom-call | flops 17179869184 | bytes 71303168 | tf_op jit(solution)/shard_map/pallas_call | solution.py:57
  78.7 2.2 copy-done
  82.2 4.8 %collective-permute-start.7 = (f16[3,2,32,4096]{3,2,1,0:T(8,128)(2,1)}, f16[3,2,32,4096]{3,2,1,0:T(8,128)(2,1)}, u32[]{:S(2)}, u32[]{:S(2)}) collective-permute-start(f16[3,2,32,4096]{3,2,1,0:T(8,128)(2,1)} %bitcast.1), channel_id=1, source_target_pairs={{0,1},{3,2},{4,5},{7,6},{8,9},{11,10},{12,13},{15,14},{16,17},{19,... | collective-permute-start | bytes 4718600 | tf_op jit(solution)/shard_map/ppermute | solution.py:81
  87.0 33.5 %shard_map.65 = f32[8,32,4096]{2,1,0:T(8,128)} custom-call(s32[8]{0:T(128)} %fusion.28.slot_ref, bf16[8,32,8192]{2,1,0:T(8,128)(2,1)} %bitcast.114, bf16[8192,4096]{1,0:T(8,128)(2,1)} %refs_1_.5, bf16[64,4096]{1,0:T(8,128)(2,1)} %bitcast.111), custom_call_target="tpu_custom_call" | custom-call | flops 17179869184 | bytes 71303168 | tf_op jit(solution)/shard_map/pallas_call | solution.py:57
  120.5 2.2 copy-done.3
  122.7 1.4 slice_convert_fusion.1
  124.1 2.4 collective-permute-start.9
  126.5 2.5 add_convert_fusion.2
  129.0 1.6 collective-permute-start.8
  131.4 28.2 %shard_map.66 = f32[8,64,2048]{2,1,0:T(8,128)} custom-call(s32[8]{0:T(128)} %fusion.28.slot_ref, bf16[8,64,8192]{2,1,0:T(8,128)(2,1)} %bitcast.105, bf16[8192,4096]{1,0:T(8,128)(2,1)} %refs_1_.5, bf16[64,4096]{1,0:T(8,128)(2,1)} %bitcast.112), custom_call_target="tpu_custom_call" | custom-call | flops 17179869184 | bytes 37748736 | tf_op jit(solution)/shard_map/pallas_call | solution.py:57
  159.6 3.4 %slice_convert_fusion = f16[6,64,2048]{2,1,0:T(8,128)(2,1)} fusion(f32[8,64,2048]{2,1,0:T(8,128)} %shard_map.66), kind=kLoop, calls=%fused_computation.1 | loop fusion | flops 786432 | bytes 4718592 | tf_op jit(solution)/shard_map/convert.12
  163.0 3.7 %collective-permute-start.12 = (f16[3,2,64,2048]{3,2,1,0:T(8,128)(2,1)}, f16[3,2,64,2048]{3,2,1,0:T(8,128)(2,1)S(1)}, u32[]{:S(2)}, u32[]{:S(2)}) collective-permute-start(f16[3,2,64,2048]{3,2,1,0:T(8,128)(2,1)} %bitcast.10), channel_id=1, source_target_pairs={{0,1},{3,2},{4,5},{7,6},{8,9},{11,10},{12,13},{15,14},{16,17},{19,... | collective-permute-start | bytes 4718600 | tf_op jit(solution)/shard_map/ppermute | solution.py:81
  166.8 2.5 add_convert_fusion.1
  170.0 2.0 fusion.17
  172.0 1.5 collective-permute-start.10
  173.4 28.3 %shard_map.67 = f32[8,64,2048]{2,1,0:T(8,128)} custom-call(s32[8]{0:T(128)} %fusion.28.slot_ref, bf16[8,64,8192]{2,1,0:T(8,128)(2,1)} %bitcast.106, bf16[8192,4096]{1,0:T(8,128)(2,1)} %refs_1_.5, bf16[64,4096]{1,0:T(8,128)(2,1)} %bitcast.113), custom_call_target="tpu_custom_call" | custom-call | flops 17179869184 | bytes 37748736 | tf_op jit(solution)/shard_map/pallas_call | solution.py:57
  201.7 2.2 fusion.26
  204.0 5.5 %collective-permute-start.16 = (f16[1,2,64,2048]{3,2,1,0:T(8,128)(2,1)S(1)}, f16[1,2,64,2048]{3,2,1,0:T(8,128)(2,1)S(1)}, u32[]{:S(2)}, u32[]{:S(2)}) collective-permute-start(f16[1,2,64,2048]{3,2,1,0:T(8,128)(2,1)S(1)} %get-tuple-element.34), channel_id=1, source_target_pairs={{0,1},{3,2},{4,5},{7,6},{8,9},{11,10},{12,13},{15,14},{16,17},{19,... | collective-permute-start | bytes 1572872 | tf_op jit(solution)/shard_map/ppermute | solution.py:81
  213.4 8.3 %collective-permute-done.16 = f16[1,2,64,2048]{3,2,1,0:T(8,128)(2,1)S(1)} collective-permute-done((f16[1,2,64,2048]{3,2,1,0:T(8,128)(2,1)S(1)}, f16[1,2,64,2048]{3,2,1,0:T(8,128)(2,1)S(1)}, u32[]{:S(2)}, u32[]{:S(2)}) %collective-permute-start.16) | collective-permute-done | bytes 524320 | tf_op jit(solution)/shard_map/ppermute | solution.py:81
  223.0 1.4 fusion.23
  224.4 8.6 %collective-permute-done.15 = f16[1,2,64,2048]{3,2,1,0:T(8,128)(2,1)S(1)} collective-permute-done((f16[1,2,64,2048]{3,2,1,0:T(8,128)(2,1)S(1)}, f16[1,2,64,2048]{3,2,1,0:T(8,128)(2,1)S(1)}, u32[]{:S(2)}, u32[]{:S(2)}) %collective-permute-start.15) | collective-permute-done | bytes 524320 | tf_op jit(solution)/shard_map/ppermute | solution.py:81
  233.6 1.4 fusion.24
  237.2 1.4 fusion.22
  239.9 2.4 fusion.21
  242.9 29.4 %collective-permute-done.21 = f16[1,2,64,2048]{3,2,1,0:T(8,128)(2,1)S(1)} collective-permute-done((f16[1,2,64,2048]{3,2,1,0:T(8,128)(2,1)S(1)}, f16[1,2,64,2048]{3,2,1,0:T(8,128)(2,1)S(1)}, u32[]{:S(2)}, u32[]{:S(2)}) %collective-permute-start.21) | collective-permute-done | bytes 524320 | tf_op jit(solution)/shard_map/ppermute | solution.py:81
  272.3 2.3 fusion.9
  274.6 2.3 maximum_maximum_fusion
  (91 shorter events, 22.3 us)
Async XLA Ops:
  6.5 31.4 %copy-start.7 = (bf16[128,8192]{1,0:T(8,128)(2,1)S(1)}, bf16[128,8192]{1,0:T(8,128)(2,1)}, u32[]{:S(2)}) copy-start(bf16[128,8192]{1,0:T(8,128)(2,1)} %param.6) | copy-start | bytes 6291460
  6.5 33.2 %copy-start.16 = (s32[64,32]{0,1:T(8,128)S(1)}, s32[64,32]{0,1:T(8,128)}, u32[]{:S(2)}) copy-start(s32[64,32]{0,1:T(8,128)} %param.8) | copy-start | bytes 24580
  6.5 80.5 %all-gather.5.cloned.1.call-start = ((), (), s32[]{:S(2)}) async-start(), calls=%async_computation | async-start | bytes 4718592 | tf_op jit(solution)/shard_map/all_gather | solution.py:158
  8.8 36.3 %copy-start.5 = (bf16[32,8192]{1,0:T(8,128)(2,1)}, bf16[32,8192]{1,0:T(8,128)(2,1)S(1)}, u32[]{:S(2)}) copy-start(bf16[32,8192]{1,0:T(8,128)(2,1)S(1)} %get-tuple-element.41.refs_0_) | copy-start | bytes 1572868
  8.8 32.5 %copy-start.17 = (f32[256]{0:T(256)S(1)}, f32[256]{0:T(256)}, u32[]{:S(2)}) copy-start(f32[256]{0:T(256)} %param.10) | copy-start | bytes 3076
  8.8 34.1 %copy-start.15 = (f32[4096]{0:T(1024)S(1)}, f32[4096]{0:T(1024)}, u32[]{:S(2)}) copy-start(f32[4096]{0:T(1024)} %param.11) | copy-start | bytes 49156
  8.8 15.7 %collective-permute-start.1 = (bf16[32,8192]{1,0:T(8,128)(2,1)S(1)}, bf16[32,8192]{1,0:T(8,128)(2,1)S(1)}, u32[]{:S(2)}, u32[]{:S(2)}) collective-permute-start(bf16[32,8192]{1,0:T(8,128)(2,1)S(1)} %get-tuple-element.41.refs_0_), channel_id=1, source_target_pairs={{0,8},{4,12},{8,0},{12,4},{16,24},{20,28},{24,16},{28,20},{1,9},{5... | collective-permute-start | bytes 1572872 | tf_op jit(solution)/shard_map/ppermute | solution.py:72
  11.7 24.6 %collective-permute-start.3 = (bf16[32,8192]{1,0:T(8,128)(2,1)S(1)}, bf16[32,8192]{1,0:T(8,128)(2,1)S(1)}, u32[]{:S(2)}, u32[]{:S(2)}) collective-permute-start(bf16[32,8192]{1,0:T(8,128)(2,1)S(1)} %get-tuple-element.41.refs_0_), channel_id=1, source_target_pairs={{0,16},{4,20},{8,24},{12,28},{16,0},{20,4},{24,8},{28,12},{1,17},{... | collective-permute-start | bytes 1572872 | tf_op jit(solution)/shard_map/ppermute | solution.py:72
  13.2 23.1 %collective-permute-start.5 = (bf16[32,8192]{1,0:T(8,128)(2,1)S(1)}, bf16[32,8192]{1,0:T(8,128)(2,1)S(1)}, u32[]{:S(2)}, u32[]{:S(2)}) collective-permute-start(bf16[32,8192]{1,0:T(8,128)(2,1)S(1)} %get-tuple-element.41.refs_0_), channel_id=1, source_target_pairs={{0,24},{4,28},{8,16},{12,20},{16,8},{20,12},{24,0},{28,4},{1,25},{... | collective-permute-start | bytes 1572872 | tf_op jit(solution)/shard_map/ppermute | solution.py:72
  24.5 20.6 %copy-start.8 = (bf16[32,8192]{1,0:T(8,128)(2,1)}, bf16[32,8192]{1,0:T(8,128)(2,1)S(1)}, u32[]{:S(2)}) copy-start(bf16[32,8192]{1,0:T(8,128)(2,1)S(1)} %collective-permute-done.1.refs_2_) | copy-start | bytes 1572868
  37.9 93.5 %all-gather.7.cloned.1.call-start = ((), (), s32[]{:S(2)}) async-start(), calls=%async_computation.1 | async-start | bytes 9437184 | tf_op jit(solution)/shard_map/all_gather | solution.py:158
  39.1 3.7 %collective-permute-start = (bf16[32,8192]{1,0:T(8,128)(2,1)S(1)}, bf16[32,8192]{1,0:T(8,128)(2,1)S(1)}, u32[]{:S(2)}, u32[]{:S(2)}) collective-permute-start(bf16[32,8192]{1,0:T(8,128)(2,1)S(1)} %get-tuple-element.41.refs_0_), channel_id=1, source_target_pairs={{0,4},{4,0},{8,12},{12,8},{16,20},{20,16},{24,28},{28,24},{1,5},{5... | collective-permute-start | bytes 1572872 | tf_op jit(solution)/shard_map/ppermute | solution.py:73
  41.3 2.0 collective-permute-start.2
  41.8 2.5 collective-permute-start.4
  41.9 3.2 %collective-permute-start.6 = (bf16[32,8192]{1,0:T(8,128)(2,1)}, bf16[32,8192]{1,0:T(8,128)(2,1)S(1)}, u32[]{:S(2)}, u32[]{:S(2)}) collective-permute-start(bf16[32,8192]{1,0:T(8,128)(2,1)} %copy-done.10), channel_id=1, source_target_pairs={{0,4},{4,0},{8,12},{12,8},{16,20},{20,16},{24,28},{28,24},{1,5},{5... | collective-permute-start | bytes 1572872 | tf_op jit(solution)/shard_map/ppermute | solution.py:75
  82.2 44.3 %collective-permute-start.7 = (f16[3,2,32,4096]{3,2,1,0:T(8,128)(2,1)}, f16[3,2,32,4096]{3,2,1,0:T(8,128)(2,1)}, u32[]{:S(2)}, u32[]{:S(2)}) collective-permute-start(f16[3,2,32,4096]{3,2,1,0:T(8,128)(2,1)} %bitcast.1), channel_id=1, source_target_pairs={{0,1},{3,2},{4,5},{7,6},{8,9},{11,10},{12,13},{15,14},{16,17},{19,... | collective-permute-start | bytes 4718600 | tf_op jit(solution)/shard_map/ppermute | solution.py:81
  124.1 42.7 %collective-permute-start.9 = (f16[3,2,32,4096]{3,2,1,0:T(8,128)(2,1)}, f16[3,2,32,4096]{3,2,1,0:T(8,128)(2,1)}, u32[]{:S(2)}, u32[]{:S(2)}) collective-permute-start(f16[3,2,32,4096]{3,2,1,0:T(8,128)(2,1)} %bitcast.5), channel_id=1, source_target_pairs={{0,1},{3,2},{4,5},{7,6},{8,9},{11,10},{12,13},{15,14},{16,17},{19,... | collective-permute-start | bytes 4718600 | tf_op jit(solution)/shard_map/ppermute | solution.py:81
  129.0 41.0 %collective-permute-start.8 = (f16[2,2,32,4096]{3,2,1,0:T(8,128)(2,1)}, f16[2,2,32,4096]{3,2,1,0:T(8,128)(2,1)}, u32[]{:S(2)}, u32[]{:S(2)}) collective-permute-start(f16[2,2,32,4096]{3,2,1,0:T(8,128)(2,1)} %add_convert_fusion.2), channel_id=1, source_target_pairs={{1,2},{2,1},{5,6},{6,5},{9,10},{10,9},{13,14},{14,13},{17,18},{18,... | collective-permute-start | bytes 3145736 | tf_op jit(solution)/shard_map/ppermute | solution.py:81
  163.0 47.7 %collective-permute-start.12 = (f16[3,2,64,2048]{3,2,1,0:T(8,128)(2,1)}, f16[3,2,64,2048]{3,2,1,0:T(8,128)(2,1)S(1)}, u32[]{:S(2)}, u32[]{:S(2)}) collective-permute-start(f16[3,2,64,2048]{3,2,1,0:T(8,128)(2,1)} %bitcast.10), channel_id=1, source_target_pairs={{0,1},{3,2},{4,5},{7,6},{8,9},{11,10},{12,13},{15,14},{16,17},{19,... | collective-permute-start | bytes 4718600 | tf_op jit(solution)/shard_map/ppermute | solution.py:81
  169.3 43.2 %collective-permute-start.11 = (f16[2,2,32,4096]{3,2,1,0:T(8,128)(2,1)}, f16[2,2,32,4096]{3,2,1,0:T(8,128)(2,1)S(1)}, u32[]{:S(2)}, u32[]{:S(2)}) collective-permute-start(f16[2,2,32,4096]{3,2,1,0:T(8,128)(2,1)} %add_convert_fusion.1), channel_id=1, source_target_pairs={{1,2},{2,1},{5,6},{6,5},{9,10},{10,9},{13,14},{14,13},{17,18},{18,... | collective-permute-start | bytes 3145736 | tf_op jit(solution)/shard_map/ppermute | solution.py:81
  172.0 66.6 %collective-permute-start.10 = (f16[1,2,32,4096]{3,2,1,0:T(8,128)(2,1)}, f16[1,2,32,4096]{3,2,1,0:T(8,128)(2,1)}, u32[]{:S(2)}, u32[]{:S(2)}) collective-permute-start(f16[1,2,32,4096]{3,2,1,0:T(8,128)(2,1)} %fusion.17), channel_id=1, source_target_pairs={{2,3},{1,0},{6,7},{5,4},{10,11},{9,8},{14,15},{13,12},{18,19},{17,... | collective-permute-start | bytes 1572872 | tf_op jit(solution)/shard_map/ppermute | solution.py:81
  204.0 17.8 %collective-permute-start.16 = (f16[1,2,64,2048]{3,2,1,0:T(8,128)(2,1)S(1)}, f16[1,2,64,2048]{3,2,1,0:T(8,128)(2,1)S(1)}, u32[]{:S(2)}, u32[]{:S(2)}) collective-permute-start(f16[1,2,64,2048]{3,2,1,0:T(8,128)(2,1)S(1)} %get-tuple-element.34), channel_id=1, source_target_pairs={{0,1},{3,2},{4,5},{7,6},{8,9},{11,10},{12,13},{15,14},{16,17},{19,... | collective-permute-start | bytes 1572872 | tf_op jit(solution)/shard_map/ppermute | solution.py:81
  209.4 23.5 %collective-permute-start.15 = (f16[1,2,64,2048]{3,2,1,0:T(8,128)(2,1)S(1)}, f16[1,2,64,2048]{3,2,1,0:T(8,128)(2,1)S(1)}, u32[]{:S(2)}, u32[]{:S(2)}) collective-permute-start(f16[1,2,64,2048]{3,2,1,0:T(8,128)(2,1)S(1)} %get-tuple-element.33), channel_id=1, source_target_pairs={{0,1},{3,2},{4,5},{7,6},{8,9},{11,10},{12,13},{15,14},{16,17},{19,... | collective-permute-start | bytes 1572872 | tf_op jit(solution)/shard_map/ppermute | solution.py:81
  210.8 32.1 %collective-permute-start.18 = (f16[1,2,64,2048]{3,2,1,0:T(8,128)(2,1)S(1)}, f16[1,2,64,2048]{3,2,1,0:T(8,128)(2,1)S(1)}, u32[]{:S(2)}, u32[]{:S(2)}) collective-permute-start(f16[1,2,64,2048]{3,2,1,0:T(8,128)(2,1)S(1)} %get-tuple-element.35), channel_id=1, source_target_pairs={{0,1},{3,2},{4,5},{7,6},{8,9},{11,10},{12,13},{15,14},{16,17},{19,... | collective-permute-start | bytes 1572872 | tf_op jit(solution)/shard_map/ppermute | solution.py:81
  212.4 23.3 %copy-start.2 = (f32[8,64,2048]{2,1,0:T(8,128)S(1)}, f32[8,64,2048]{2,1,0:T(8,128)}, u32[]{:S(2)}) copy-start(f32[8,64,2048]{2,1,0:T(8,128)} %shard_map.66) | copy-start | bytes 12582916
  212.4 22.6 %collective-permute-start.14 = (f16[2,2,64,2048]{3,2,1,0:T(8,128)(2,1)S(1)}, f16[2,2,64,2048]{3,2,1,0:T(8,128)(2,1)S(1)}, u32[]{:S(2)}, u32[]{:S(2)}) collective-permute-start(f16[2,2,64,2048]{3,2,1,0:T(8,128)(2,1)S(1)} %add_convert_fusion), channel_id=1, source_target_pairs={{1,2},{2,1},{5,6},{6,5},{9,10},{10,9},{13,14},{14,13},{17,18},{18,... | collective-permute-start | bytes 3145736 | tf_op jit(solution)/shard_map/ppermute | solution.py:81
  221.7 18.2 %collective-permute-start.13 = (f16[1,2,32,4096]{3,2,1,0:T(8,128)(2,1)S(1)}, f16[1,2,32,4096]{3,2,1,0:T(8,128)(2,1)S(1)}, u32[]{:S(2)}, u32[]{:S(2)}) collective-permute-start(f16[1,2,32,4096]{3,2,1,0:T(8,128)(2,1)S(1)} %fusion.11), channel_id=1, source_target_pairs={{2,3},{1,0},{6,7},{5,4},{10,11},{9,8},{14,15},{13,12},{18,19},{17,... | collective-permute-start | bytes 1572872 | tf_op jit(solution)/shard_map/ppermute | solution.py:81
  224.4 15.5 %copy-start.6 = (bf16[256,4096]{1,0:T(8,128)(2,1)S(1)}, bf16[256,4096]{1,0:T(8,128)(2,1)}, u32[]{:S(2)}) copy-start(bf16[256,4096]{1,0:T(8,128)(2,1)} %param.9) | copy-start | bytes 6291460
  233.0 2.9 %collective-permute-start.20 = (f16[1,2,64,2048]{3,2,1,0:T(8,128)(2,1)S(1)}, f16[1,2,64,2048]{3,2,1,0:T(8,128)(2,1)S(1)}, u32[]{:S(2)}, u32[]{:S(2)}) collective-permute-start(f16[1,2,64,2048]{3,2,1,0:T(8,128)(2,1)S(1)} %fusion.23), channel_id=1, source_target_pairs={{1,2},{2,1},{5,6},{6,5},{9,10},{10,9},{13,14},{14,13},{17,18},{18,... | collective-permute-start | bytes 1572872 | tf_op jit(solution)/shard_map/ppermute | solution.py:81
  235.0 7.8 %collective-permute-start.19 = (f16[1,2,64,2048]{3,2,1,0:T(8,128)(2,1)S(1)}, f16[1,2,64,2048]{3,2,1,0:T(8,128)(2,1)S(1)}, u32[]{:S(2)}, u32[]{:S(2)}) collective-permute-start(f16[1,2,64,2048]{3,2,1,0:T(8,128)(2,1)S(1)} %fusion.24), channel_id=1, source_target_pairs={{1,2},{2,1},{5,6},{6,5},{9,10},{10,9},{13,14},{14,13},{17,18},{18,... | collective-permute-start | bytes 1572872 | tf_op jit(solution)/shard_map/ppermute | solution.py:81
  235.9 36.4 %collective-permute-start.17 = (f16[1,2,64,2048]{3,2,1,0:T(8,128)(2,1)S(1)}, f16[1,2,64,2048]{3,2,1,0:T(8,128)(2,1)S(1)}, u32[]{:S(2)}, u32[]{:S(2)}) collective-permute-start(f16[1,2,64,2048]{3,2,1,0:T(8,128)(2,1)S(1)} %fusion.5), channel_id=1, source_target_pairs={{2,3},{1,0},{6,7},{5,4},{10,11},{9,8},{14,15},{13,12},{18,19},{17,... | collective-permute-start | bytes 1572872 | tf_op jit(solution)/shard_map/ppermute | solution.py:81
  238.6 33.7 %collective-permute-start.21 = (f16[1,2,64,2048]{3,2,1,0:T(8,128)(2,1)S(1)}, f16[1,2,64,2048]{3,2,1,0:T(8,128)(2,1)S(1)}, u32[]{:S(2)}, u32[]{:S(2)}) collective-permute-start(f16[1,2,64,2048]{3,2,1,0:T(8,128)(2,1)S(1)} %fusion.22), channel_id=1, source_target_pairs={{2,3},{1,0},{6,7},{5,4},{10,11},{9,8},{14,15},{13,12},{18,19},{17,... | collective-permute-start | bytes 1572872 | tf_op jit(solution)/shard_map/ppermute | solution.py:81
  (13 other events, 45.7 us)
Sparse Core Ops, SparseCore 0:
  38.1 37.0 all-gather.4
  77.0 54.3 all-gather.6

commit v2 on v1

--- a/solution.py
+++ b/solution.py
@@ -9,9 +9,9 @@
 MIB = 2**20
 
 
-def product_kernel(pieces, waits, slot_ref, *refs):
+def product_kernel(pieces, slot_ref, *refs):
     sources = refs[: len(pieces)]
-    integrals_ref, mask_ref, out_ref, rows, masked, sems = refs[len(pieces) + waits :]
+    integrals_ref, mask_ref, out_ref, rows, masked, sems = refs[len(pieces) :]
 
     @pl.when(pl.program_id(0) == 0)
     def _():
@@ -35,14 +35,14 @@
     out_ref[...] = total.reshape(out_ref.shape)
 
 
-def product(arrays, slots, integrals, mask, first, width, block, waits):
+def product(arrays, slots, integrals, mask, first, width, block):
     m, depth = arrays[0].shape[-2:]
     pieces = [a.shape[0] if a.ndim == 3 else 1 for a in arrays]
     devices, tiles = sum(pieces), mask.shape[0]
     grid_spec = pltpu.PrefetchScalarGridSpec(
         num_scalar_prefetch=1,
         grid=(width // block,),
-        in_specs=[pl.BlockSpec(memory_space=pl.ANY)] * (len(arrays) + len(waits))
+        in_specs=[pl.BlockSpec(memory_space=pl.ANY)] * len(arrays)
         + [
             pl.BlockSpec((depth, block), lambda n, s: (0, first // block + n)),
             pl.BlockSpec((tiles, block), lambda n, s: (0, first // block + n)),
@@ -55,7 +55,7 @@
         ],
     )
     return pl.pallas_call(
-        functools.partial(product_kernel, pieces, len(waits)),
+        functools.partial(product_kernel, pieces),
         grid_spec=grid_spec,
         out_shape=jax.ShapeDtypeStruct((devices, m, width), jnp.float32),
         compiler_params=pltpu.CompilerParams(vmem_limit_bytes=56 * MIB),
@@ -64,14 +64,15 @@
             bytes_accessed=2 * depth * width + 4 * devices * m * width,
             transcendentals=0,
         ),
-    )(slots, *arrays, *waits, integrals, mask)
+    )(slots, *arrays, integrals, mask)
 
 
 def gather(own, rows):
     swap = [(i, i ^ 1) for i in range(rows)]
-    others = [lax.ppermute(own, "row", [(i, i ^ q) for i in range(rows)]) for q in range(2, rows, 2)]
     pieces = [own, lax.ppermute(own, "row", swap)]
-    for other in others:
+    for q in range(2, rows, 2):
+        other = lax.ppermute(own, "row", [(i, i ^ q) for i in range(rows)])
+        other = after(other, pieces[1:2])
         pieces += [other, lax.ppermute(other, "row", swap)]
     return pieces
 
@@ -123,8 +124,8 @@
 
 def plan(local):
     if local == 128:
-        return ((32, False, 1), (32, True, 1), (64, True, 2))
-    return ((local, True, 1),)
+        return ((16, False, (8,)), (48, True, (8,)), (64, True, (4, 4)))
+    return ((local, True, (8,)),)
 
 
 def shards(rows, cols, amplitudes, integrals, tile_mask, driving, occupied_energy, virtual_energy):
@@ -148,24 +149,24 @@
     driving = driving.reshape(share, local, width)
     occupied = occupied_energy.reshape(share, local, 1)
     layout = plan(local)
-    count = sum(chunks for _, _, chunks in layout)
-    chains, order, begun, offset, where = [], [], [], 0, []
+    count = sum(len(chunks) for _, _, chunks in layout)
+    chains, order, offset, where = [], [], 0, []
     for m, whole, chunks in layout:
         part = slice(offset, offset + m)
         offset += m
-        own = after(amplitudes[part], begun)
+        own = amplitudes[part]
         if whole:
             arrays, slots = [lax.all_gather(own, "row", axis=0)], slots_all
         else:
             arrays, slots = gather(own, rows), slots_xor
-            begun = arrays[2::2]
-        chunk = width // chunks
-        for c in range(chunks):
-            at = c * chunk
-            sums = product(arrays, after(slots, order), integrals, mask, at, chunk, min(chunk, 512), [])
+        at = 0
+        for eighths in chunks:
+            chunk = width * eighths // 8
+            sums = product(arrays, after(slots, order), integrals, mask, at, chunk, min(chunk, 512))
             split = cols == 4 and len(chains) == count - 1
             chains.append(Chain(sums.reshape(cols, share, m, chunk), cols, split))
             where.append((part, slice(at, at + chunk)))
+            at += chunk
             for edge, chain in enumerate(chains[: -cols : -1]):
                 order = chain.advance(edge, order)
     for late in range(1, cols - 1):

time: 284 us -> 277 us (0.975)
  other arithmetic: 28 us -> 23.5 us
    ppermute x15, waiting for transfers between devices: 46.8 us -> 53.1 us  [send(): return lax.ppermute(values, 'col', pairs)]
    ppermute x3, waiting for transfers between devices: 23.1 us -> 16.9 us  [gather(): other = lax.ppermute(own, 'row', [(i, i ^ q) for i in range(rows)])]
    convert_element_type x10, other arithmetic: 13.8 us -> 7.92 us  [advance(): values = values.astype(jnp.float16)]
    unnamed x37 -> x47, local copies, waits for them, and re-layouts: 7.79 us -> 4.99 us
  transfers between devices with their start and end apart: 24 -> 24, of which waited for: 10 -> 8; matrix products, arithmetic and copies ran while one was open for 9% -> 8% of each run, Pallas kernels for 43% -> 45%
where the time goes in v2:
time: 277 us; the launch traced here: 276 us
  Pallas kernels  124 us (45%)
  waiting for transfers between devices  72.4 us (26%)
  starting transfers between devices  32.9 us (12%)
  other arithmetic  23.5 us (8%)
  between operations  13.9 us (5%)
  local copies, waits for them, and re-layouts  8.9 us (3%)
    pallas_call x4, Pallas kernels, product(): pl.pallas_call(functools.partial(product_kernel, pieces), grid_spec=grid_...  124 us
    ppermute x15, waiting for transfers between devices, send(): return lax.ppermute(values, 'col', pairs)  53.1 us
    ppermute x15, starting transfers between devices, send(): return lax.ppermute(values, 'col', pairs)  27.7 us
    ppermute x3, waiting for transfers between devices, gather(): other = lax.ppermute(own, 'row', [(i, i ^ q) for i in range(rows)])  16.9 us
    convert_element_type x10, other arithmetic, advance(): values = values.astype(jnp.float16)  7.92 us
    another operation x3, other arithmetic  7.71 us
  transfers between devices with their start and end apart: 24, of which 8 were waited for; matrix products, arithmetic and copies ran while one was open for 8% of the time, Pallas kernels for 45%

profile of v2, /device:TPU:0, one launch (start us, length us, event | category | flops | bytes accessed | tf_op | source)
XLA Modules:
  0.0 276.1 jit_solution(11431637074832547462)
XLA Ops:
  6.5 2.2 slice.168
  10.5 2.6 collective-permute-start.3
  13.1 1.4 collective-permute-start.5
  15.3 14.1 %collective-permute-done.3.refs_4_ = bf16[16,8192]{1,0:T(8,128)(2,1)S(1)} collective-permute-done((bf16[16,8192]{1,0:T(8,128)(2,1)S(1)}, bf16[16,8192]{1,0:T(8,128)(2,1)S(1)}, u32[]{:S(2)}, u32[]{:S(2)}) %collective-permute-start.3) | collective-permute-done | bytes 262176 | tf_op jit(solution)/shard_map/ppermute | solution.py:74
  30.0 2.7 collective-permute-done.1.refs_2_
  35.6 27.6 %shard_map.64 = f32[8,16,4096]{2,1,0:T(8,128)} custom-call(s32[8]{0:T(128)} %fusion.29.slot_ref, bf16[16,8192]{1,0:T(8,128)(2,1)} %copy-done.7, bf16[16,8192]{1,0:T(8,128)(2,1)} %copy-done.11, bf16[16,8192]{1,0:T(8,128)(2,1)} %copy-done.14, bf16[16,8192]{1,0:T(8,128)(2,1)} %copy-done.17, bf16[16,8192]{1,0:T(8,128)(2,1)} %copy-done.12, ...), custom_call_target="tpu_custom_call" | custom-call | flops 8589934592 | bytes 69206016 | tf_op jit(solution)/shard_map/pallas_call | solution.py:57
  63.2 1.6 copy-done.2
  64.9 3.2 %collective-permute-start.7 = (f16[3,2,16,4096]{3,2,1,0:T(8,128)(2,1)S(1)}, f16[3,2,16,4096]{3,2,1,0:T(8,128)(2,1)S(1)}, u32[]{:S(2)}, u32[]{:S(2)}) collective-permute-start(f16[3,2,16,4096]{3,2,1,0:T(8,128)(2,1)S(1)} %bitcast.120), channel_id=1, source_target_pairs={{0,1},{3,2},{4,5},{7,6},{8,9},{11,10},{12,13},{15,14},{16,17},{19,... | collective-permute-start | bytes 2359304 | tf_op jit(solution)/shard_map/ppermute | solution.py:82
  68.1 40.4 %shard_map.65 = f32[8,48,4096]{2,1,0:T(8,128)} custom-call(s32[8]{0:T(128)} %fusion.28.slot_ref, bf16[8,48,8192]{2,1,0:T(8,128)(2,1)} %bitcast.124, bf16[8192,4096]{1,0:T(8,128)(2,1)} %refs_1_.5, bf16[64,4096]{1,0:T(8,128)(2,1)} %bitcast.113), custom_call_target="tpu_custom_call" | custom-call | flops 25769803776 | bytes 73400320 | tf_op jit(solution)/shard_map/pallas_call | solution.py:57
  108.5 4.2 %slice_convert_fusion = f16[6,48,4096]{2,1,0:T(8,128)(2,1)} fusion(f32[8,48,4096]{2,1,0:T(8,128)} %shard_map.65), kind=kLoop, calls=%fused_computation | loop fusion | flops 1179648 | bytes 7077888 | tf_op jit(solution)/shard_map/convert.13
  112.7 2.7 collective-permute-start.9
  117.1 2.4 all-gather.7.cloned.1.call-done
  119.5 28.2 %shard_map.66 = f32[8,64,2048]{2,1,0:T(8,128)} custom-call(s32[8]{0:T(128)} %fusion.28.slot_ref, bf16[8,64,8192]{2,1,0:T(8,128)(2,1)} %bitcast.105, bf16[8192,4096]{1,0:T(8,128)(2,1)} %refs_1_.5, bf16[64,4096]{1,0:T(8,128)(2,1)} %bitcast.114), custom_call_target="tpu_custom_call" | custom-call | flops 17179869184 | bytes 37748736 | tf_op jit(solution)/shard_map/pallas_call | solution.py:57
  147.7 3.4 %slice_convert_fusion.1 = f16[6,64,2048]{2,1,0:T(8,128)(2,1)} fusion(f32[8,64,2048]{2,1,0:T(8,128)} %shard_map.66), kind=kLoop, calls=%fused_computation.2 | loop fusion | flops 786432 | bytes 4718592 | tf_op jit(solution)/shard_map/convert.12
  151.1 14.4 %collective-permute-done.9 = f16[3,2,48,4096]{3,2,1,0:T(8,128)(2,1)} collective-permute-done((f16[3,2,48,4096]{3,2,1,0:T(8,128)(2,1)}, f16[3,2,48,4096]{3,2,1,0:T(8,128)(2,1)}, u32[]{:S(2)}, u32[]{:S(2)}) %collective-permute-start.9) | collective-permute-done | bytes 2359328 | tf_op jit(solution)/shard_map/ppermute | solution.py:82
  165.5 3.2 %add_convert_fusion = f16[2,2,48,4096]{3,2,1,0:T(8,128)(2,1)} fusion(f32[2,2,48,4096]{3,2,1,0:T(8,128)S(1)} %bitcast.110, f16[3,2,48,4096]{3,2,1,0:T(8,128)(2,1)} %collective-permute-done.9), kind=kLoop, calls=%fused_computation.3 | loop fusion | flops 2359296 | bytes 6291456 | tf_op jit(solution)/shard_map/convert_element_type | solution.py:109
  169.4 1.5 collective-permute-start.10
  171.0 5.5 %collective-permute-start.12 = (f16[3,2,64,2048]{3,2,1,0:T(8,128)(2,1)}, f16[3,2,64,2048]{3,2,1,0:T(8,128)(2,1)S(1)}, u32[]{:S(2)}, u32[]{:S(2)}) collective-permute-start(f16[3,2,64,2048]{3,2,1,0:T(8,128)(2,1)} %bitcast.10), channel_id=1, source_target_pairs={{0,1},{3,2},{4,5},{7,6},{8,9},{11,10},{12,13},{15,14},{16,17},{19,... | collective-permute-start | bytes 4718600 | tf_op jit(solution)/shard_map/ppermute | solution.py:82
  176.5 1.8 collective-permute-start.11
  178.3 28.2 %shard_map.67 = f32[8,64,2048]{2,1,0:T(8,128)} custom-call(s32[8]{0:T(128)} %fusion.28.slot_ref, bf16[8,64,8192]{2,1,0:T(8,128)(2,1)} %bitcast.106, bf16[8192,4096]{1,0:T(8,128)(2,1)} %refs_1_.5, bf16[64,4096]{1,0:T(8,128)(2,1)} %bitcast.115), custom_call_target="tpu_custom_call" | custom-call | flops 17179869184 | bytes 37748736 | tf_op jit(solution)/shard_map/pallas_call | solution.py:57
  206.6 2.1 fusion.20
  208.7 3.4 %collective-permute-start.16 = (f16[1,2,64,2048]{3,2,1,0:T(8,128)(2,1)S(1)}, f16[1,2,64,2048]{3,2,1,0:T(8,128)(2,1)S(1)}, u32[]{:S(2)}, u32[]{:S(2)}) collective-permute-start(f16[1,2,64,2048]{3,2,1,0:T(8,128)(2,1)S(1)} %get-tuple-element.36), channel_id=1, source_target_pairs={{0,1},{3,2},{4,5},{7,6},{8,9},{11,10},{12,13},{15,14},{16,17},{19,... | collective-permute-start | bytes 1572872 | tf_op jit(solution)/shard_map/ppermute | solution.py:82
  212.2 1.4 collective-permute-start.15
  213.6 1.3 collective-permute-start.18
  217.5 1.5 fusion.1
  219.0 1.3 collective-permute-start.13
  220.3 4.2 %collective-permute-done.16 = f16[1,2,64,2048]{3,2,1,0:T(8,128)(2,1)S(1)} collective-permute-done((f16[1,2,64,2048]{3,2,1,0:T(8,128)(2,1)S(1)}, f16[1,2,64,2048]{3,2,1,0:T(8,128)(2,1)S(1)}, u32[]{:S(2)}, u32[]{:S(2)}) %collective-permute-start.16) | collective-permute-done | bytes 524320 | tf_op jit(solution)/shard_map/ppermute | solution.py:82
  225.4 10.4 %collective-permute-done.15 = f16[1,2,64,2048]{3,2,1,0:T(8,128)(2,1)S(1)} collective-permute-done((f16[1,2,64,2048]{3,2,1,0:T(8,128)(2,1)S(1)}, f16[1,2,64,2048]{3,2,1,0:T(8,128)(2,1)S(1)}, u32[]{:S(2)}, u32[]{:S(2)}) %collective-permute-start.15) | collective-permute-done | bytes 524320 | tf_op jit(solution)/shard_map/ppermute | solution.py:82
  239.6 2.0 fusion.5
  241.6 3.7 %collective-permute-done.18 = f16[1,2,64,2048]{3,2,1,0:T(8,128)(2,1)S(1)} collective-permute-done((f16[1,2,64,2048]{3,2,1,0:T(8,128)(2,1)S(1)}, f16[1,2,64,2048]{3,2,1,0:T(8,128)(2,1)S(1)}, u32[]{:S(2)}, u32[]{:S(2)}) %collective-permute-start.18) | collective-permute-done | bytes 524320 | tf_op jit(solution)/shard_map/ppermute | solution.py:82
  245.3 20.4 %collective-permute-done.21 = f16[1,2,64,2048]{3,2,1,0:T(8,128)(2,1)S(1)} collective-permute-done((f16[1,2,64,2048]{3,2,1,0:T(8,128)(2,1)S(1)}, f16[1,2,64,2048]{3,2,1,0:T(8,128)(2,1)S(1)}, u32[]{:S(2)}, u32[]{:S(2)}) %collective-permute-start.21) | collective-permute-done | bytes 524320 | tf_op jit(solution)/shard_map/ppermute | solution.py:82
  266.8 2.5 maximum_maximum_fusion
  (105 shorter events, 16.5 us)
Async XLA Ops:
  6.5 61.6 %all-gather.5.cloned.1.call-start = ((), (), s32[]{:S(2)}) async-start(), calls=%async_computation | async-start | bytes 7077888 | tf_op jit(solution)/shard_map/all_gather | solution.py:159
  8.8 24.5 %copy-start.19 = (s32[64,32]{0,1:T(8,128)S(1)}, s32[64,32]{0,1:T(8,128)}, u32[]{:S(2)}) copy-start(s32[64,32]{0,1:T(8,128)} %param.8) | copy-start | bytes 24580
  8.8 110.7 %all-gather.7.cloned.1.call-start = ((), (), s32[]{:S(2)}) async-start(), calls=%async_computation.1 | async-start | bytes 9437184 | tf_op jit(solution)/shard_map/all_gather | solution.py:159
  9.9 24.8 %copy-start.18 = (f32[4096]{0:T(1024)S(1)}, f32[4096]{0:T(1024)}, u32[]{:S(2)}) copy-start(f32[4096]{0:T(1024)} %param.11) | copy-start | bytes 49156
  10.0 24.8 %copy-start.7 = (bf16[16,8192]{1,0:T(8,128)(2,1)}, bf16[16,8192]{1,0:T(8,128)(2,1)S(1)}, u32[]{:S(2)}) copy-start(bf16[16,8192]{1,0:T(8,128)(2,1)S(1)} %slice.162.refs_0_) | copy-start | bytes 786436
  10.0 5.3 %collective-permute-start = (bf16[16,8192]{1,0:T(8,128)(2,1)S(1)}, bf16[16,8192]{1,0:T(8,128)(2,1)S(1)}, u32[]{:S(2)}, u32[]{:S(2)}) collective-permute-start(bf16[16,8192]{1,0:T(8,128)(2,1)S(1)} %slice.162.refs_0_), channel_id=1, source_target_pairs={{0,4},{4,0},{8,12},{12,8},{16,20},{20,16},{24,28},{28,24},{1,5},{5... | collective-permute-start | bytes 786440 | tf_op jit(solution)/shard_map/ppermute | solution.py:72
  10.5 19.0 %collective-permute-start.3 = (bf16[16,8192]{1,0:T(8,128)(2,1)S(1)}, bf16[16,8192]{1,0:T(8,128)(2,1)S(1)}, u32[]{:S(2)}, u32[]{:S(2)}) collective-permute-start(bf16[16,8192]{1,0:T(8,128)(2,1)S(1)} %slice.162.refs_0_), channel_id=1, source_target_pairs={{0,16},{4,20},{8,24},{12,28},{16,0},{20,4},{24,8},{28,12},{1,17},{... | collective-permute-start | bytes 786440 | tf_op jit(solution)/shard_map/ppermute | solution.py:74
  13.1 16.4 %collective-permute-start.5 = (bf16[16,8192]{1,0:T(8,128)(2,1)S(1)}, bf16[16,8192]{1,0:T(8,128)(2,1)S(1)}, u32[]{:S(2)}, u32[]{:S(2)}) collective-permute-start(bf16[16,8192]{1,0:T(8,128)(2,1)S(1)} %slice.162.refs_0_), channel_id=1, source_target_pairs={{0,24},{4,28},{8,16},{12,20},{16,8},{20,12},{24,0},{28,4},{1,25},{... | collective-permute-start | bytes 786440 | tf_op jit(solution)/shard_map/ppermute | solution.py:74
  14.5 18.2 %collective-permute-start.1 = (bf16[16,8192]{1,0:T(8,128)(2,1)S(1)}, bf16[16,8192]{1,0:T(8,128)(2,1)S(1)}, u32[]{:S(2)}, u32[]{:S(2)}) collective-permute-start(bf16[16,8192]{1,0:T(8,128)(2,1)S(1)} %slice.162.refs_0_), channel_id=1, source_target_pairs={{0,8},{4,12},{8,0},{12,4},{16,24},{20,28},{24,16},{28,20},{1,9},{5... | collective-permute-start | bytes 786440 | tf_op jit(solution)/shard_map/ppermute | solution.py:74
  15.3 19.5 %copy-start.11 = (bf16[16,8192]{1,0:T(8,128)(2,1)}, bf16[16,8192]{1,0:T(8,128)(2,1)S(1)}, u32[]{:S(2)}) copy-start(bf16[16,8192]{1,0:T(8,128)(2,1)S(1)} %collective-permute-done.refs_1_) | copy-start | bytes 786436
  29.5 5.3 %collective-permute-start.4 = (bf16[16,8192]{1,0:T(8,128)(2,1)S(1)}, bf16[16,8192]{1,0:T(8,128)(2,1)S(1)}, u32[]{:S(2)}, u32[]{:S(2)}) collective-permute-start(bf16[16,8192]{1,0:T(8,128)(2,1)S(1)} %collective-permute-done.3.refs_4_), channel_id=1, source_target_pairs={{0,4},{4,0},{8,12},{12,8},{16,20},{20,16},{24,28},{28,24},{1,5},{5... | collective-permute-start | bytes 786440 | tf_op jit(solution)/shard_map/ppermute | solution.py:76
  29.5 5.3 %collective-permute-start.6 = (bf16[16,8192]{1,0:T(8,128)(2,1)S(1)}, bf16[16,8192]{1,0:T(8,128)(2,1)S(1)}, u32[]{:S(2)}, u32[]{:S(2)}) collective-permute-start(bf16[16,8192]{1,0:T(8,128)(2,1)S(1)} %collective-permute-done.5.refs_6_), channel_id=1, source_target_pairs={{0,4},{4,0},{8,12},{12,8},{16,20},{20,16},{24,28},{28,24},{1,5},{5... | collective-permute-start | bytes 786440 | tf_op jit(solution)/shard_map/ppermute | solution.py:76
  32.7 2.1 collective-permute-start.2
  64.9 50.6 %collective-permute-start.7 = (f16[3,2,16,4096]{3,2,1,0:T(8,128)(2,1)S(1)}, f16[3,2,16,4096]{3,2,1,0:T(8,128)(2,1)S(1)}, u32[]{:S(2)}, u32[]{:S(2)}) collective-permute-start(f16[3,2,16,4096]{3,2,1,0:T(8,128)(2,1)S(1)} %bitcast.120), channel_id=1, source_target_pairs={{0,1},{3,2},{4,5},{7,6},{8,9},{11,10},{12,13},{15,14},{16,17},{19,... | collective-permute-start | bytes 2359304 | tf_op jit(solution)/shard_map/ppermute | solution.py:82
  112.7 52.7 %collective-permute-start.9 = (f16[3,2,48,4096]{3,2,1,0:T(8,128)(2,1)}, f16[3,2,48,4096]{3,2,1,0:T(8,128)(2,1)}, u32[]{:S(2)}, u32[]{:S(2)}) collective-permute-start(f16[3,2,48,4096]{3,2,1,0:T(8,128)(2,1)} %bitcast.5), channel_id=1, source_target_pairs={{0,1},{3,2},{4,5},{7,6},{8,9},{11,10},{12,13},{15,14},{16,17},{19,... | collective-permute-start | bytes 7077896 | tf_op jit(solution)/shard_map/ppermute | solution.py:82
  116.4 52.2 %collective-permute-start.8 = (f16[2,2,16,4096]{3,2,1,0:T(8,128)(2,1)S(1)}, f16[2,2,16,4096]{3,2,1,0:T(8,128)(2,1)S(1)}, u32[]{:S(2)}, u32[]{:S(2)}) collective-permute-start(f16[2,2,16,4096]{3,2,1,0:T(8,128)(2,1)S(1)} %add_convert_fusion.2), channel_id=1, source_target_pairs={{1,2},{2,1},{5,6},{6,5},{9,10},{10,9},{13,14},{14,13},{17,18},{18,... | collective-permute-start | bytes 1572872 | tf_op jit(solution)/shard_map/ppermute | solution.py:82
  147.7 17.8 %slice-start.3 = ((f32[8,48,4096]{2,1,0:T(8,128)}), f32[4,48,4096]{2,1,0:T(8,128)S(1)}, s32[]{:S(2)}) async-start(f32[8,48,4096]{2,1,0:T(8,128)} %shard_map.65), calls=%async_computation.5 | async-start | bytes 6291456 | tf_op jit(solution)/shard_map/slice | solution.py:102
  165.5 52.0 %slice-start.1 = ((s8[6291456]{0:T(1024)(128)(4,1)}), s8[2097152]{0:T(1024)(128)(4,1)S(1)}, s32[]{:S(2)}) async-start(s8[6291456]{0:T(1024)(128)(4,1)} %bitcast.108), calls=%async_computation.3 | async-start | bytes 4194304
  169.4 48.0 %slice-start.2 = ((s8[6291456]{0:T(1024)(128)(4,1)}), s8[4194304]{0:T(1024)(128)(4,1)S(1)}, s32[]{:S(2)}) async-start(s8[6291456]{0:T(1024)(128)(4,1)} %bitcast.108), calls=%async_computation.4 | async-start | bytes 8388608
  169.4 44.2 %collective-permute-start.10 = (f16[1,2,16,4096]{3,2,1,0:T(8,128)(2,1)S(1)}, f16[1,2,16,4096]{3,2,1,0:T(8,128)(2,1)}, u32[]{:S(2)}, u32[]{:S(2)}) collective-permute-start(f16[1,2,16,4096]{3,2,1,0:T(8,128)(2,1)S(1)} %fusion.23), channel_id=1, source_target_pairs={{2,3},{1,0},{6,7},{5,4},{10,11},{9,8},{14,15},{13,12},{18,19},{17,... | collective-permute-start | bytes 786440 | tf_op jit(solution)/shard_map/ppermute | solution.py:82
  171.0 45.2 %collective-permute-start.12 = (f16[3,2,64,2048]{3,2,1,0:T(8,128)(2,1)}, f16[3,2,64,2048]{3,2,1,0:T(8,128)(2,1)S(1)}, u32[]{:S(2)}, u32[]{:S(2)}) collective-permute-start(f16[3,2,64,2048]{3,2,1,0:T(8,128)(2,1)} %bitcast.10), channel_id=1, source_target_pairs={{0,1},{3,2},{4,5},{7,6},{8,9},{11,10},{12,13},{15,14},{16,17},{19,... | collective-permute-start | bytes 4718600 | tf_op jit(solution)/shard_map/ppermute | solution.py:82
  176.5 41.0 %collective-permute-start.11 = (f16[2,2,48,4096]{3,2,1,0:T(8,128)(2,1)}, f16[2,2,48,4096]{3,2,1,0:T(8,128)(2,1)}, u32[]{:S(2)}, u32[]{:S(2)}) collective-permute-start(f16[2,2,48,4096]{3,2,1,0:T(8,128)(2,1)} %add_convert_fusion), channel_id=1, source_target_pairs={{1,2},{2,1},{5,6},{6,5},{9,10},{10,9},{13,14},{14,13},{17,18},{18,... | collective-permute-start | bytes 4718600 | tf_op jit(solution)/shard_map/ppermute | solution.py:82
  208.7 15.8 %collective-permute-start.16 = (f16[1,2,64,2048]{3,2,1,0:T(8,128)(2,1)S(1)}, f16[1,2,64,2048]{3,2,1,0:T(8,128)(2,1)S(1)}, u32[]{:S(2)}, u32[]{:S(2)}) collective-permute-start(f16[1,2,64,2048]{3,2,1,0:T(8,128)(2,1)S(1)} %get-tuple-element.36), channel_id=1, source_target_pairs={{0,1},{3,2},{4,5},{7,6},{8,9},{11,10},{12,13},{15,14},{16,17},{19,... | collective-permute-start | bytes 1572872 | tf_op jit(solution)/shard_map/ppermute | solution.py:82
  212.2 23.6 %collective-permute-start.15 = (f16[1,2,64,2048]{3,2,1,0:T(8,128)(2,1)S(1)}, f16[1,2,64,2048]{3,2,1,0:T(8,128)(2,1)S(1)}, u32[]{:S(2)}, u32[]{:S(2)}) collective-permute-start(f16[1,2,64,2048]{3,2,1,0:T(8,128)(2,1)S(1)} %get-tuple-element.35), channel_id=1, source_target_pairs={{0,1},{3,2},{4,5},{7,6},{8,9},{11,10},{12,13},{15,14},{16,17},{19,... | collective-permute-start | bytes 1572872 | tf_op jit(solution)/shard_map/ppermute | solution.py:82
  213.6 31.7 %collective-permute-start.18 = (f16[1,2,64,2048]{3,2,1,0:T(8,128)(2,1)S(1)}, f16[1,2,64,2048]{3,2,1,0:T(8,128)(2,1)S(1)}, u32[]{:S(2)}, u32[]{:S(2)}) collective-permute-start(f16[1,2,64,2048]{3,2,1,0:T(8,128)(2,1)S(1)} %get-tuple-element.37), channel_id=1, source_target_pairs={{0,1},{3,2},{4,5},{7,6},{8,9},{11,10},{12,13},{15,14},{16,17},{19,... | collective-permute-start | bytes 1572872 | tf_op jit(solution)/shard_map/ppermute | solution.py:82
  216.6 20.0 %collective-permute-start.14 = (f16[2,2,64,2048]{3,2,1,0:T(8,128)(2,1)S(1)}, f16[2,2,64,2048]{3,2,1,0:T(8,128)(2,1)S(1)}, u32[]{:S(2)}, u32[]{:S(2)}) collective-permute-start(f16[2,2,64,2048]{3,2,1,0:T(8,128)(2,1)S(1)} %add_convert_fusion.1), channel_id=1, source_target_pairs={{1,2},{2,1},{5,6},{6,5},{9,10},{10,9},{13,14},{14,13},{17,18},{18,... | collective-permute-start | bytes 3145736 | tf_op jit(solution)/shard_map/ppermute | solution.py:82
  217.5 19.1 %copy-start = (f32[8,64,2048]{2,1,0:T(8,128)S(1)}, f32[8,64,2048]{2,1,0:T(8,128)}, u32[]{:S(2)}) copy-start(f32[8,64,2048]{2,1,0:T(8,128)} %shard_map.66) | copy-start | bytes 12582916
  219.0 20.6 %collective-permute-start.13 = (f16[1,2,48,4096]{3,2,1,0:T(8,128)(2,1)S(1)}, f16[1,2,48,4096]{3,2,1,0:T(8,128)(2,1)S(1)}, u32[]{:S(2)}, u32[]{:S(2)}) collective-permute-start(f16[1,2,48,4096]{3,2,1,0:T(8,128)(2,1)S(1)} %fusion.1), channel_id=1, source_target_pairs={{2,3},{1,0},{6,7},{5,4},{10,11},{9,8},{14,15},{13,12},{18,19},{17,... | collective-permute-start | bytes 2359304 | tf_op jit(solution)/shard_map/ppermute | solution.py:82
  224.7 13.4 %collective-permute-start.20 = (f16[1,2,64,2048]{3,2,1,0:T(8,128)(2,1)S(1)}, f16[1,2,64,2048]{3,2,1,0:T(8,128)(2,1)S(1)}, u32[]{:S(2)}, u32[]{:S(2)}) collective-permute-start(f16[1,2,64,2048]{3,2,1,0:T(8,128)(2,1)S(1)} %fusion.17), channel_id=1, source_target_pairs={{1,2},{2,1},{5,6},{6,5},{9,10},{10,9},{13,14},{14,13},{17,18},{18,... | collective-permute-start | bytes 1572872 | tf_op jit(solution)/shard_map/ppermute | solution.py:82
  235.9 9.4 %collective-permute-start.19 = (f16[1,2,64,2048]{3,2,1,0:T(8,128)(2,1)S(1)}, f16[1,2,64,2048]{3,2,1,0:T(8,128)(2,1)S(1)}, u32[]{:S(2)}, u32[]{:S(2)}) collective-permute-start(f16[1,2,64,2048]{3,2,1,0:T(8,128)(2,1)S(1)} %fusion.18), channel_id=1, source_target_pairs={{1,2},{2,1},{5,6},{6,5},{9,10},{10,9},{13,14},{14,13},{17,18},{18,... | collective-permute-start | bytes 1572872 | tf_op jit(solution)/shard_map/ppermute | solution.py:82
  236.8 28.9 %collective-permute-start.17 = (f16[1,2,64,2048]{3,2,1,0:T(8,128)(2,1)S(1)}, f16[1,2,64,2048]{3,2,1,0:T(8,128)(2,1)S(1)}, u32[]{:S(2)}, u32[]{:S(2)}) collective-permute-start(f16[1,2,64,2048]{3,2,1,0:T(8,128)(2,1)S(1)} %fusion.11), channel_id=1, source_target_pairs={{2,3},{1,0},{6,7},{5,4},{10,11},{9,8},{14,15},{13,12},{18,19},{17,... | collective-permute-start | bytes 1572872 | tf_op jit(solution)/shard_map/ppermute | solution.py:82
  238.3 27.5 %collective-permute-start.21 = (f16[1,2,64,2048]{3,2,1,0:T(8,128)(2,1)S(1)}, f16[1,2,64,2048]{3,2,1,0:T(8,128)(2,1)S(1)}, u32[]{:S(2)}, u32[]{:S(2)}) collective-permute-start(f16[1,2,64,2048]{3,2,1,0:T(8,128)(2,1)S(1)} %fusion.16), channel_id=1, source_target_pairs={{2,3},{1,0},{6,7},{5,4},{10,11},{9,8},{14,15},{13,12},{18,19},{17,... | collective-permute-start | bytes 1572872 | tf_op jit(solution)/shard_map/ppermute | solution.py:82
  (18 other events, 73.5 us)
Sparse Core Ops, SparseCore 0:
  9.2 53.8 all-gather.4
  65.0 54.3 all-gather.6

commit v3 on v2

--- a/solution.py
+++ b/solution.py
@@ -124,7 +124,7 @@
 
 def plan(local):
     if local == 128:
-        return ((16, False, (8,)), (48, True, (8,)), (64, True, (4, 4)))
+        return ((16, False, (8,)), (48, True, (4, 4)), (64, True, (4, 4)))
     return ((local, True, (8,)),)
 
 

time: 277 us -> 292 us (1.054)
  starting transfers between devices: 32.9 us -> 44.9 us
  Pallas kernels: 124 us -> 133 us
  waiting for transfers between devices: 72.4 us -> 65.2 us
    ppermute x15 -> x18, starting transfers between devices: 27.7 us -> 39.8 us  [send(): return lax.ppermute(values, 'col', pairs)]
    pallas_call x4 -> x5, Pallas kernels: 124 us -> 133 us  [product(): pl.pallas_call(functools.partial(product_kernel, pieces), grid_spec=grid_...]
    ppermute x15 -> x18, waiting for transfers between devices: 53.1 us -> 49.1 us  [send(): return lax.ppermute(values, 'col', pairs)]
    convert_element_type x10 -> x12, other arithmetic: 7.92 us -> 8.93 us  [advance(): values = values.astype(jnp.float16)]
    another operation x3 -> x4, other arithmetic: 7.71 us -> 8.41 us
  transfers between devices with their start and end apart: 24 -> 27, of which waited for: 8 -> 8; matrix products, arithmetic and copies ran while one was open for 8% -> 8% of each run, Pallas kernels for 45% -> 46%
where the time goes in v3:
time: 292 us; the launch traced here: 291 us
  Pallas kernels  133 us (46%)
  waiting for transfers between devices  65.2 us (22%)
  starting transfers between devices  44.9 us (15%)
  other arithmetic  25.2 us (9%)
  between operations  14 us (5%)
  local copies, waits for them, and re-layouts  9.15 us (3%)
    pallas_call x5, Pallas kernels, product(): pl.pallas_call(functools.partial(product_kernel, pieces), grid_spec=grid_...  133 us
    ppermute x18, waiting for transfers between devices, send(): return lax.ppermute(values, 'col', pairs)  49.1 us
    ppermute x18, starting transfers between devices, send(): return lax.ppermute(values, 'col', pairs)  39.8 us
    ppermute x3, waiting for transfers between devices, gather(): other = lax.ppermute(own, 'row', [(i, i ^ q) for i in range(rows)])  16 us
    convert_element_type x12, other arithmetic, advance(): values = values.astype(jnp.float16)  8.93 us
    another operation x4, other arithmetic  8.41 us
  transfers between devices with their start and end apart: 27, of which 8 were waited for; matrix products, arithmetic and copies ran while one was open for 8% of the time, Pallas kernels for 46%

profile of v3, /device:TPU:0, one launch (start us, length us, event | category | flops | bytes accessed | tf_op | source)
XLA Modules:
  0.0 291.3 jit_solution(11168767099815365839)
XLA Ops:
  6.5 2.2 slice.207
  10.0 4.0 %collective-permute-start.5 = (bf16[16,8192]{1,0:T(8,128)(2,1)S(1)}, bf16[16,8192]{1,0:T(8,128)(2,1)S(1)}, u32[]{:S(2)}, u32[]{:S(2)}) collective-permute-start(bf16[16,8192]{1,0:T(8,128)(2,1)S(1)} %slice.201.refs_0_), channel_id=1, source_target_pairs={{0,24},{4,28},{8,16},{12,20},{16,8},{20,12},{24,0},{28,4},{1,25},{... | collective-permute-start | bytes 786440 | tf_op jit(solution)/shard_map/ppermute | solution.py:74
  15.2 5.9 %collective-permute-done.5.refs_6_ = bf16[16,8192]{1,0:T(8,128)(2,1)S(1)} collective-permute-done((bf16[16,8192]{1,0:T(8,128)(2,1)S(1)}, bf16[16,8192]{1,0:T(8,128)(2,1)S(1)}, u32[]{:S(2)}, u32[]{:S(2)}) %collective-permute-start.5) | collective-permute-done | bytes 262176 | tf_op jit(solution)/shard_map/ppermute | solution.py:74
  21.1 8.4 %collective-permute-done.3.refs_4_ = bf16[16,8192]{1,0:T(8,128)(2,1)S(1)} collective-permute-done((bf16[16,8192]{1,0:T(8,128)(2,1)S(1)}, bf16[16,8192]{1,0:T(8,128)(2,1)S(1)}, u32[]{:S(2)}, u32[]{:S(2)}) %collective-permute-start.3) | collective-permute-done | bytes 262176 | tf_op jit(solution)/shard_map/ppermute | solution.py:74
  29.6 1.6 collective-permute-done.1.refs_2_
  34.7 28.2 %shard_map.64 = f32[8,16,4096]{2,1,0:T(8,128)} custom-call(s32[8]{0:T(128)} %fusion.35.slot_ref, bf16[16,8192]{1,0:T(8,128)(2,1)} %copy-done.9, bf16[16,8192]{1,0:T(8,128)(2,1)} %copy-done.14, bf16[16,8192]{1,0:T(8,128)(2,1)} %copy-done.13, bf16[16,8192]{1,0:T(8,128)(2,1)} %copy-done.15, bf16[16,8192]{1,0:T(8,128)(2,1)} %copy-done.12, ...), custom_call_target="tpu_custom_call" | custom-call | flops 8589934592 | bytes 69206016 | tf_op jit(solution)/shard_map/pallas_call | solution.py:57
  62.9 1.6 copy-done.4
  64.6 3.2 %collective-permute-start.7 = (f16[3,2,16,4096]{3,2,1,0:T(8,128)(2,1)S(1)}, f16[3,2,16,4096]{3,2,1,0:T(8,128)(2,1)S(1)}, u32[]{:S(2)}, u32[]{:S(2)}) collective-permute-start(f16[3,2,16,4096]{3,2,1,0:T(8,128)(2,1)S(1)} %bitcast.144), channel_id=1, source_target_pairs={{0,1},{3,2},{4,5},{7,6},{8,9},{11,10},{12,13},{15,14},{16,17},{19,... | collective-permute-start | bytes 2359304 | tf_op jit(solution)/shard_map/ppermute | solution.py:82
  67.8 24.4 %shard_map.65 = f32[8,48,2048]{2,1,0:T(8,128)} custom-call(s32[8]{0:T(128)} %fusion.34.slot_ref, bf16[8,48,8192]{2,1,0:T(8,128)(2,1)} %bitcast.129, bf16[8192,4096]{1,0:T(8,128)(2,1)} %refs_1_.7, bf16[64,4096]{1,0:T(8,128)(2,1)} %bitcast.134), custom_call_target="tpu_custom_call" | custom-call | flops 12884901888 | bytes 36700160 | tf_op jit(solution)/shard_map/pallas_call | solution.py:57
  92.3 1.9 slice_convert_fusion.2
  95.1 5.0 %collective-permute-start.9 = (f16[3,2,48,2048]{3,2,1,0:T(8,128)(2,1)S(1)}, f16[3,2,48,2048]{3,2,1,0:T(8,128)(2,1)S(1)}, u32[]{:S(2)}, u32[]{:S(2)}) collective-permute-start(f16[3,2,48,2048]{3,2,1,0:T(8,128)(2,1)S(1)} %bitcast.143), channel_id=1, source_target_pairs={{0,1},{3,2},{4,5},{7,6},{8,9},{11,10},{12,13},{15,14},{16,17},{19,... | collective-permute-start | bytes 3538952 | tf_op jit(solution)/shard_map/ppermute | solution.py:82
  100.1 23.8 %shard_map.66 = f32[8,48,2048]{2,1,0:T(8,128)} custom-call(s32[8]{0:T(128)} %fusion.34.slot_ref, bf16[8,48,8192]{2,1,0:T(8,128)(2,1)} %bitcast.130, bf16[8192,4096]{1,0:T(8,128)(2,1)} %refs_1_.7, bf16[64,4096]{1,0:T(8,128)(2,1)} %bitcast.135), custom_call_target="tpu_custom_call" | custom-call | flops 12884901888 | bytes 36700160 | tf_op jit(solution)/shard_map/pallas_call | solution.py:57
  123.9 3.0 %slice_convert_fusion.1 = f16[6,48,2048]{2,1,0:T(8,128)(2,1)} fusion(f32[8,48,2048]{2,1,0:T(8,128)} %shard_map.66), kind=kLoop, calls=%fused_computation.2 | loop fusion | flops 589824 | bytes 3538944 | tf_op jit(solution)/shard_map/convert.16
  130.6 5.6 %collective-permute-start.12 = (f16[3,2,48,2048]{3,2,1,0:T(8,128)(2,1)}, f16[3,2,48,2048]{3,2,1,0:T(8,128)(2,1)}, u32[]{:S(2)}, u32[]{:S(2)}) collective-permute-start(f16[3,2,48,2048]{3,2,1,0:T(8,128)(2,1)} %bitcast.9), channel_id=1, source_target_pairs={{0,1},{3,2},{4,5},{7,6},{8,9},{11,10},{12,13},{15,14},{16,17},{19,... | collective-permute-start | bytes 3538952 | tf_op jit(solution)/shard_map/ppermute | solution.py:82
  136.3 1.5 collective-permute-start.11
  137.8 2.0 collective-permute-done.10
  141.1 28.2 %shard_map.67 = f32[8,64,2048]{2,1,0:T(8,128)} custom-call(s32[8]{0:T(128)} %fusion.34.slot_ref, bf16[8,64,8192]{2,1,0:T(8,128)(2,1)} %bitcast.126, bf16[8192,4096]{1,0:T(8,128)(2,1)} %refs_1_.7, bf16[64,4096]{1,0:T(8,128)(2,1)} %bitcast.136), custom_call_target="tpu_custom_call" | custom-call | flops 17179869184 | bytes 37748736 | tf_op jit(solution)/shard_map/pallas_call | solution.py:57
  169.3 3.4 %slice_convert_fusion = f16[6,64,2048]{2,1,0:T(8,128)(2,1)} fusion(f32[8,64,2048]{2,1,0:T(8,128)} %shard_map.67), kind=kLoop, calls=%fused_computation.1 | loop fusion | flops 786432 | bytes 4718592 | tf_op jit(solution)/shard_map/convert.15
  172.7 1.5 add_convert_fusion.1
  174.8 1.8 fusion.20
  177.9 1.6 collective-permute-start.14
  179.5 6.2 %collective-permute-start.15 = (f16[3,2,64,2048]{3,2,1,0:T(8,128)(2,1)}, f16[3,2,64,2048]{3,2,1,0:T(8,128)(2,1)S(1)}, u32[]{:S(2)}, u32[]{:S(2)}) collective-permute-start(f16[3,2,64,2048]{3,2,1,0:T(8,128)(2,1)} %bitcast.18), channel_id=1, source_target_pairs={{0,1},{3,2},{4,5},{7,6},{8,9},{11,10},{12,13},{15,14},{16,17},{19,... | collective-permute-start | bytes 4718600 | tf_op jit(solution)/shard_map/ppermute | solution.py:82
  185.7 28.3 %shard_map.68 = f32[8,64,2048]{2,1,0:T(8,128)} custom-call(s32[8]{0:T(128)} %fusion.34.slot_ref, bf16[8,64,8192]{2,1,0:T(8,128)(2,1)} %bitcast.127, bf16[8192,4096]{1,0:T(8,128)(2,1)} %refs_1_.7, bf16[64,4096]{1,0:T(8,128)(2,1)} %bitcast.137), custom_call_target="tpu_custom_call" | custom-call | flops 17179869184 | bytes 37748736 | tf_op jit(solution)/shard_map/pallas_call | solution.py:57
  214.0 2.1 fusion.26
  216.1 1.6 collective-permute-start.18
  219.0 1.7 collective-permute-done.15
  220.7 4.3 %collective-permute-start.21 = (f16[1,2,64,2048]{3,2,1,0:T(8,128)(2,1)S(1)}, f16[1,2,64,2048]{3,2,1,0:T(8,128)(2,1)S(1)}, u32[]{:S(2)}, u32[]{:S(2)}) collective-permute-start(f16[1,2,64,2048]{3,2,1,0:T(8,128)(2,1)S(1)} %get-tuple-element.43), channel_id=1, source_target_pairs={{0,1},{3,2},{4,5},{7,6},{8,9},{11,10},{12,13},{15,14},{16,17},{19,... | collective-permute-start | bytes 1572872 | tf_op jit(solution)/shard_map/ppermute | solution.py:82
  227.6 15.5 %collective-permute-done.19 = f16[1,2,64,2048]{3,2,1,0:T(8,128)(2,1)S(1)} collective-permute-done((f16[1,2,64,2048]{3,2,1,0:T(8,128)(2,1)S(1)}, f16[1,2,64,2048]{3,2,1,0:T(8,128)(2,1)S(1)}, u32[]{:S(2)}, u32[]{:S(2)}) %collective-permute-start.19) | collective-permute-done | bytes 524320 | tf_op jit(solution)/shard_map/ppermute | solution.py:82
  249.1 4.0 %collective-permute-done.16 = f16[1,2,48,2048]{3,2,1,0:T(8,128)(2,1)S(1)} collective-permute-done((f16[1,2,48,2048]{3,2,1,0:T(8,128)(2,1)S(1)}, f16[1,2,48,2048]{3,2,1,0:T(8,128)(2,1)S(1)}, u32[]{:S(2)}, u32[]{:S(2)}) %collective-permute-start.16) | collective-permute-done | bytes 393248 | tf_op jit(solution)/shard_map/ppermute | solution.py:82
  253.1 2.2 fusion.24
  255.4 25.8 %collective-permute-done.24 = f16[1,2,64,2048]{3,2,1,0:T(8,128)(2,1)S(1)} collective-permute-done((f16[1,2,64,2048]{3,2,1,0:T(8,128)(2,1)S(1)}, f16[1,2,64,2048]{3,2,1,0:T(8,128)(2,1)S(1)}, u32[]{:S(2)}, u32[]{:S(2)}) %collective-permute-start.24) | collective-permute-done | bytes 524320 | tf_op jit(solution)/shard_map/ppermute | solution.py:82
  282.2 2.3 maximum_maximum_fusion
  (112 shorter events, 24.3 us)
Async XLA Ops:
  6.5 61.3 %all-gather.5.cloned.1.call-start = ((), (), s32[]{:S(2)}) async-start(), calls=%async_computation | async-start | bytes 7077888 | tf_op jit(solution)/shard_map/all_gather | solution.py:159
  8.8 23.5 %copy-start.19 = (s32[64,32]{0,1:T(8,128)S(1)}, s32[64,32]{0,1:T(8,128)}, u32[]{:S(2)}) copy-start(s32[64,32]{0,1:T(8,128)} %param.8) | copy-start | bytes 24580
  8.8 132.2 %all-gather.7.cloned.1.call-start = ((), (), s32[]{:S(2)}) async-start(), calls=%async_computation.1 | async-start | bytes 9437184 | tf_op jit(solution)/shard_map/all_gather | solution.py:159
  10.0 23.9 %copy-start.9 = (bf16[16,8192]{1,0:T(8,128)(2,1)}, bf16[16,8192]{1,0:T(8,128)(2,1)S(1)}, u32[]{:S(2)}) copy-start(bf16[16,8192]{1,0:T(8,128)(2,1)S(1)} %slice.201.refs_0_) | copy-start | bytes 786436
  10.0 11.1 %collective-permute-start.5 = (bf16[16,8192]{1,0:T(8,128)(2,1)S(1)}, bf16[16,8192]{1,0:T(8,128)(2,1)S(1)}, u32[]{:S(2)}, u32[]{:S(2)}) collective-permute-start(bf16[16,8192]{1,0:T(8,128)(2,1)S(1)} %slice.201.refs_0_), channel_id=1, source_target_pairs={{0,24},{4,28},{8,16},{12,20},{16,8},{20,12},{24,0},{28,4},{1,25},{... | collective-permute-start | bytes 786440 | tf_op jit(solution)/shard_map/ppermute | solution.py:74
  13.9 15.6 %collective-permute-start.3 = (bf16[16,8192]{1,0:T(8,128)(2,1)S(1)}, bf16[16,8192]{1,0:T(8,128)(2,1)S(1)}, u32[]{:S(2)}, u32[]{:S(2)}) collective-permute-start(bf16[16,8192]{1,0:T(8,128)(2,1)S(1)} %slice.201.refs_0_), channel_id=1, source_target_pairs={{0,16},{4,20},{8,24},{12,28},{16,0},{20,4},{24,8},{28,12},{1,17},{... | collective-permute-start | bytes 786440 | tf_op jit(solution)/shard_map/ppermute | solution.py:74
  14.5 16.8 %collective-permute-start.1 = (bf16[16,8192]{1,0:T(8,128)(2,1)S(1)}, bf16[16,8192]{1,0:T(8,128)(2,1)S(1)}, u32[]{:S(2)}, u32[]{:S(2)}) collective-permute-start(bf16[16,8192]{1,0:T(8,128)(2,1)S(1)} %slice.201.refs_0_), channel_id=1, source_target_pairs={{0,8},{4,12},{8,0},{12,4},{16,24},{20,28},{24,16},{28,20},{1,9},{5... | collective-permute-start | bytes 786440 | tf_op jit(solution)/shard_map/ppermute | solution.py:74
  14.6 6.5 %collective-permute-start = (bf16[16,8192]{1,0:T(8,128)(2,1)S(1)}, bf16[16,8192]{1,0:T(8,128)(2,1)S(1)}, u32[]{:S(2)}, u32[]{:S(2)}) collective-permute-start(bf16[16,8192]{1,0:T(8,128)(2,1)S(1)} %slice.201.refs_0_), channel_id=1, source_target_pairs={{0,4},{4,0},{8,12},{12,8},{16,20},{20,16},{24,28},{28,24},{1,5},{5... | collective-permute-start | bytes 786440 | tf_op jit(solution)/shard_map/ppermute | solution.py:72
  21.1 12.7 %copy-start.14 = (bf16[16,8192]{1,0:T(8,128)(2,1)}, bf16[16,8192]{1,0:T(8,128)(2,1)S(1)}, u32[]{:S(2)}) copy-start(bf16[16,8192]{1,0:T(8,128)(2,1)S(1)} %collective-permute-done.refs_1_) | copy-start | bytes 786436
  31.2 2.6 collective-permute-start.2
  31.2 2.6 collective-permute-start.4
  31.7 2.1 collective-permute-start.6
  64.6 29.6 %collective-permute-start.7 = (f16[3,2,16,4096]{3,2,1,0:T(8,128)(2,1)S(1)}, f16[3,2,16,4096]{3,2,1,0:T(8,128)(2,1)S(1)}, u32[]{:S(2)}, u32[]{:S(2)}) collective-permute-start(f16[3,2,16,4096]{3,2,1,0:T(8,128)(2,1)S(1)} %bitcast.144), channel_id=1, source_target_pairs={{0,1},{3,2},{4,5},{7,6},{8,9},{11,10},{12,13},{15,14},{16,17},{19,... | collective-permute-start | bytes 2359304 | tf_op jit(solution)/shard_map/ppermute | solution.py:82
  94.4 33.7 %collective-permute-start.8 = (f16[2,2,16,4096]{3,2,1,0:T(8,128)(2,1)S(1)}, f16[2,2,16,4096]{3,2,1,0:T(8,128)(2,1)S(1)}, u32[]{:S(2)}, u32[]{:S(2)}) collective-permute-start(f16[2,2,16,4096]{3,2,1,0:T(8,128)(2,1)S(1)} %add_convert_fusion.3), channel_id=1, source_target_pairs={{1,2},{2,1},{5,6},{6,5},{9,10},{10,9},{13,14},{14,13},{17,18},{18,... | collective-permute-start | bytes 1572872 | tf_op jit(solution)/shard_map/ppermute | solution.py:82
  95.1 31.8 %collective-permute-start.9 = (f16[3,2,48,2048]{3,2,1,0:T(8,128)(2,1)S(1)}, f16[3,2,48,2048]{3,2,1,0:T(8,128)(2,1)S(1)}, u32[]{:S(2)}, u32[]{:S(2)}) collective-permute-start(f16[3,2,48,2048]{3,2,1,0:T(8,128)(2,1)S(1)} %bitcast.143), channel_id=1, source_target_pairs={{0,1},{3,2},{4,5},{7,6},{8,9},{11,10},{12,13},{15,14},{16,17},{19,... | collective-permute-start | bytes 3538952 | tf_op jit(solution)/shard_map/ppermute | solution.py:82
  129.3 10.5 %collective-permute-start.10 = (f16[1,2,16,4096]{3,2,1,0:T(8,128)(2,1)S(1)}, f16[1,2,16,4096]{3,2,1,0:T(8,128)(2,1)S(1)}, u32[]{:S(2)}, u32[]{:S(2)}) collective-permute-start(f16[1,2,16,4096]{3,2,1,0:T(8,128)(2,1)S(1)} %fusion.29), channel_id=1, source_target_pairs={{2,3},{1,0},{6,7},{5,4},{10,11},{9,8},{14,15},{13,12},{18,19},{17,... | collective-permute-start | bytes 786440 | tf_op jit(solution)/shard_map/ppermute | solution.py:82
  130.6 42.0 %collective-permute-start.12 = (f16[3,2,48,2048]{3,2,1,0:T(8,128)(2,1)}, f16[3,2,48,2048]{3,2,1,0:T(8,128)(2,1)}, u32[]{:S(2)}, u32[]{:S(2)}) collective-permute-start(f16[3,2,48,2048]{3,2,1,0:T(8,128)(2,1)} %bitcast.9), channel_id=1, source_target_pairs={{0,1},{3,2},{4,5},{7,6},{8,9},{11,10},{12,13},{15,14},{16,17},{19,... | collective-permute-start | bytes 3538952 | tf_op jit(solution)/shard_map/ppermute | solution.py:82
  136.3 37.9 %collective-permute-start.11 = (f16[2,2,48,2048]{3,2,1,0:T(8,128)(2,1)}, f16[2,2,48,2048]{3,2,1,0:T(8,128)(2,1)}, u32[]{:S(2)}, u32[]{:S(2)}) collective-permute-start(f16[2,2,48,2048]{3,2,1,0:T(8,128)(2,1)} %add_convert_fusion.2), channel_id=1, source_target_pairs={{1,2},{2,1},{5,6},{6,5},{9,10},{10,9},{13,14},{14,13},{17,18},{18,... | collective-permute-start | bytes 2359304 | tf_op jit(solution)/shard_map/ppermute | solution.py:82
  176.6 71.2 %collective-permute-start.13 = (f16[1,2,48,2048]{3,2,1,0:T(8,128)(2,1)}, f16[1,2,48,2048]{3,2,1,0:T(8,128)(2,1)}, u32[]{:S(2)}, u32[]{:S(2)}) collective-permute-start(f16[1,2,48,2048]{3,2,1,0:T(8,128)(2,1)} %fusion.20), channel_id=1, source_target_pairs={{2,3},{1,0},{6,7},{5,4},{10,11},{9,8},{14,15},{13,12},{18,19},{17,... | collective-permute-start | bytes 1179656 | tf_op jit(solution)/shard_map/ppermute | solution.py:82
  177.9 47.5 %collective-permute-start.14 = (f16[2,2,48,2048]{3,2,1,0:T(8,128)(2,1)S(1)}, f16[2,2,48,2048]{3,2,1,0:T(8,128)(2,1)}, u32[]{:S(2)}, u32[]{:S(2)}) collective-permute-start(f16[2,2,48,2048]{3,2,1,0:T(8,128)(2,1)S(1)} %add_convert_fusion.1), channel_id=1, source_target_pairs={{1,2},{2,1},{5,6},{6,5},{9,10},{10,9},{13,14},{14,13},{17,18},{18,... | collective-permute-start | bytes 2359304 | tf_op jit(solution)/shard_map/ppermute | solution.py:82
  179.5 41.2 %collective-permute-start.15 = (f16[3,2,64,2048]{3,2,1,0:T(8,128)(2,1)}, f16[3,2,64,2048]{3,2,1,0:T(8,128)(2,1)S(1)}, u32[]{:S(2)}, u32[]{:S(2)}) collective-permute-start(f16[3,2,64,2048]{3,2,1,0:T(8,128)(2,1)} %bitcast.18), channel_id=1, source_target_pairs={{0,1},{3,2},{4,5},{7,6},{8,9},{11,10},{12,13},{15,14},{16,17},{19,... | collective-permute-start | bytes 4718600 | tf_op jit(solution)/shard_map/ppermute | solution.py:82
  216.1 28.5 %collective-permute-start.18 = (f16[1,2,64,2048]{3,2,1,0:T(8,128)(2,1)S(1)}, f16[1,2,64,2048]{3,2,1,0:T(8,128)(2,1)S(1)}, u32[]{:S(2)}, u32[]{:S(2)}) collective-permute-start(f16[1,2,64,2048]{3,2,1,0:T(8,128)(2,1)S(1)} %get-tuple-element.41), channel_id=1, source_target_pairs={{0,1},{3,2},{4,5},{7,6},{8,9},{11,10},{12,13},{15,14},{16,17},{19,... | collective-permute-start | bytes 1572872 | tf_op jit(solution)/shard_map/ppermute | solution.py:82
  217.7 25.4 %collective-permute-start.19 = (f16[1,2,64,2048]{3,2,1,0:T(8,128)(2,1)S(1)}, f16[1,2,64,2048]{3,2,1,0:T(8,128)(2,1)S(1)}, u32[]{:S(2)}, u32[]{:S(2)}) collective-permute-start(f16[1,2,64,2048]{3,2,1,0:T(8,128)(2,1)S(1)} %get-tuple-element.42), channel_id=1, source_target_pairs={{0,1},{3,2},{4,5},{7,6},{8,9},{11,10},{12,13},{15,14},{16,17},{19,... | collective-permute-start | bytes 1572872 | tf_op jit(solution)/shard_map/ppermute | solution.py:82
  220.7 34.6 %collective-permute-start.21 = (f16[1,2,64,2048]{3,2,1,0:T(8,128)(2,1)S(1)}, f16[1,2,64,2048]{3,2,1,0:T(8,128)(2,1)S(1)}, u32[]{:S(2)}, u32[]{:S(2)}) collective-permute-start(f16[1,2,64,2048]{3,2,1,0:T(8,128)(2,1)S(1)} %get-tuple-element.43), channel_id=1, source_target_pairs={{0,1},{3,2},{4,5},{7,6},{8,9},{11,10},{12,13},{15,14},{16,17},{19,... | collective-permute-start | bytes 1572872 | tf_op jit(solution)/shard_map/ppermute | solution.py:82
  225.1 19.3 %copy-start.1 = (f32[8,64,2048]{2,1,0:T(8,128)S(1)}, f32[8,64,2048]{2,1,0:T(8,128)}, u32[]{:S(2)}) copy-start(f32[8,64,2048]{2,1,0:T(8,128)} %shard_map.68) | copy-start | bytes 12582916
  225.4 20.0 %collective-permute-start.17 = (f16[2,2,64,2048]{3,2,1,0:T(8,128)(2,1)S(1)}, f16[2,2,64,2048]{3,2,1,0:T(8,128)(2,1)S(1)}, u32[]{:S(2)}, u32[]{:S(2)}) collective-permute-start(f16[2,2,64,2048]{3,2,1,0:T(8,128)(2,1)S(1)} %add_convert_fusion), channel_id=1, source_target_pairs={{1,2},{2,1},{5,6},{6,5},{9,10},{10,9},{13,14},{14,13},{17,18},{18,... | collective-permute-start | bytes 3145736 | tf_op jit(solution)/shard_map/ppermute | solution.py:82
  226.3 19.9 %copy-start = (f32[8,64,2048]{2,1,0:T(8,128)S(1)}, f32[8,64,2048]{2,1,0:T(8,128)}, u32[]{:S(2)}) copy-start(f32[8,64,2048]{2,1,0:T(8,128)} %shard_map.67) | copy-start | bytes 12582916
  243.1 10.0 %collective-permute-start.16 = (f16[1,2,48,2048]{3,2,1,0:T(8,128)(2,1)S(1)}, f16[1,2,48,2048]{3,2,1,0:T(8,128)(2,1)S(1)}, u32[]{:S(2)}, u32[]{:S(2)}) collective-permute-start(f16[1,2,48,2048]{3,2,1,0:T(8,128)(2,1)S(1)} %fusion.14), channel_id=1, source_target_pairs={{2,3},{1,0},{6,7},{5,4},{10,11},{9,8},{14,15},{13,12},{18,19},{17,... | collective-permute-start | bytes 1179656 | tf_op jit(solution)/shard_map/ppermute | solution.py:82
  244.6 1.7 collective-permute-start.23
  245.4 9.9 %collective-permute-start.22 = (f16[1,2,64,2048]{3,2,1,0:T(8,128)(2,1)S(1)}, f16[1,2,64,2048]{3,2,1,0:T(8,128)(2,1)S(1)}, u32[]{:S(2)}, u32[]{:S(2)}) collective-permute-start(f16[1,2,64,2048]{3,2,1,0:T(8,128)(2,1)S(1)} %fusion.12), channel_id=1, source_target_pairs={{1,2},{2,1},{5,6},{6,5},{9,10},{10,9},{13,14},{14,13},{17,18},{18,... | collective-permute-start | bytes 1572872 | tf_op jit(solution)/shard_map/ppermute | solution.py:82
  246.3 34.8 %collective-permute-start.20 = (f16[1,2,64,2048]{3,2,1,0:T(8,128)(2,1)S(1)}, f16[1,2,64,2048]{3,2,1,0:T(8,128)(2,1)S(1)}, u32[]{:S(2)}, u32[]{:S(2)}) collective-permute-start(f16[1,2,64,2048]{3,2,1,0:T(8,128)(2,1)S(1)} %fusion.5), channel_id=1, source_target_pairs={{2,3},{1,0},{6,7},{5,4},{10,11},{9,8},{14,15},{13,12},{18,19},{17,... | collective-permute-start | bytes 1572872 | tf_op jit(solution)/shard_map/ppermute | solution.py:82
  247.8 33.3 %collective-permute-start.24 = (f16[1,2,64,2048]{3,2,1,0:T(8,128)(2,1)S(1)}, f16[1,2,64,2048]{3,2,1,0:T(8,128)(2,1)S(1)}, u32[]{:S(2)}, u32[]{:S(2)}) collective-permute-start(f16[1,2,64,2048]{3,2,1,0:T(8,128)(2,1)S(1)} %fusion.10), channel_id=1, source_target_pairs={{2,3},{1,0},{6,7},{5,4},{10,11},{9,8},{14,15},{13,12},{18,19},{17,... | collective-permute-start | bytes 1572872 | tf_op jit(solution)/shard_map/ppermute | solution.py:82
  (20 other events, 88.2 us)
Sparse Core Ops, SparseCore 0:
  9.2 52.1 all-gather.4
  63.3 54.3 all-gather.6
